TPU v7x, 256 devices: a whole 4x4x8 slice. The times are simulated.
256 devices in a mesh: row: 16 (over z_hi, x), col: 16 (over z_lo, y, core).
Axes of the slice: x: 4, y: 4, z: 8 (z_hi: 4, z_lo: 2; z = z_hi * 2 + z_lo), core: 2. Of those that a mesh axis runs over, the one named last changes fastest.
Arguments:
- density: float32 [16, 16, 18, 128, 128], P('row', 'col'), as said below
- tile_coords: int32 [16, 16, 18, 2], replicated, may hold values from 0 to 511, as said below
Outputs:
- purified: float32 [16, 16, 18, 128, 128], P('row', 'col')
- mean_diagonal: float32 [], replicated
Inputs may be any that keep to these rules, and one draw needn't show every extreme that they name: `tile_coords`: slot t of device (r, c) names a block (I, J) with (I div (size of axis col)) mod (size of axis row) = r and c = pi(J mod (size of axis col)) for one permutation pi of 0 to (size of axis col) - 1, the same for all blocks; every slot is filled. Each present block is named once. Block (I, J) is present exactly when (J - I) mod 512 lies in a set of 9 offsets that holds 0 and is closed under negation, so the pattern is symmetric and every block row holds 9 blocks. No device names two blocks of one block row. density[r, c, t] is the block named by tile_coords[r, c, t]; the blocks form a symmetric matrix (block (J, I) is the transpose of block (I, J)).
All inputs are finite; a program needn't handle non-finite values.
Results may differ from a plain program's by a relative error of at most 0.025.
Values may be sent and summed in bfloat16 or wider, within the bound.
A program may use at most 128 MiB of HBM per device.

v0:
```python
import jax
import jax.numpy as jnp
from jax import lax
from jax.sharding import PartitionSpec as P

NB = 512


def pair_lookup(own_coords, targets, mirror_coords):
    own_rows = own_coords[:, 0]
    own_cols = own_coords[:, 1]
    target_row = targets[:, 0]
    target_col = targets[:, 1]
    first = (own_rows[None, :] == target_row[:, None]) & (target_row[:, None] >= 0)
    has_first = jnp.any(first, axis=1)
    left_slot = jnp.argmax(first.astype(jnp.int32), axis=1)
    inner = own_cols[left_slot]
    second = (mirror_coords[None, :, 0] == target_col[:, None]) & (
        mirror_coords[None, :, 1] == inner[:, None]
    )
    second = second & has_first[:, None]
    keep = jnp.any(second, axis=1)
    right_slot = jnp.argmax(second.astype(jnp.int32), axis=1)
    return (left_slot, right_slot, keep)


def scattered_product(left, mirror, left_slot, right_slot, keep):
    weight = keep.astype(jnp.float32)
    left_rows = jnp.take(left, left_slot, axis=0)
    right_rows = jnp.take(mirror, right_slot, axis=0)
    result = jnp.einsum("nik,njk->nij", left_rows, right_rows, preferred_element_type=jnp.float32)
    return lax.psum_scatter(
        (result * weight[:, None, None]).astype(jnp.bfloat16),
        "col",
        scatter_dimension=0,
        tiled=True,
    ).astype(jnp.float32)


def per_device(density, tile_coords):
    own_tiles = density[0, 0]
    own_low = own_tiles.astype(jnp.bfloat16)
    my_row = lax.axis_index("row")
    my_col = lax.axis_index("col")
    row_table = jnp.take(tile_coords, my_row, axis=0)
    own_coords = jnp.take(row_table, my_col, axis=0)
    col_table = jnp.take(tile_coords, my_col, axis=1)
    row_flat = row_table.reshape(-1, 2)
    col_flat = col_table.reshape(-1, 2)
    mirror = lax.all_gather(own_low, "row", axis=0, tiled=True)
    own_diag = (own_coords[:, 0] == own_coords[:, 1]) & (own_coords[:, 0] >= 0)
    left_slot, right_slot, keep = pair_lookup(own_coords, row_flat, col_flat)
    square = scattered_product(own_low, mirror, left_slot, right_slot, keep)
    square_low = square.astype(jnp.bfloat16)
    cube = scattered_product(square_low, mirror, left_slot, right_slot, keep)
    purified = 3.0 * square - 2.0 * cube
    order_total = own_tiles.shape[-1] * NB
    total = lax.psum(
        jnp.sum(jnp.where(own_diag, jnp.einsum("nii->n", purified), 0.0)), ("row", "col")
    )
    mean_diagonal = total / order_total
    return (purified[None, None], mean_diagonal)


def solution(mesh):
    return jax.shard_map(
        per_device,
        mesh=mesh,
        in_specs=(P("row", "col", None, None, None), P()),
        out_specs=(P("row", "col", None, None, None), P()),
        check_vma=False,
    )
```

profile of v0, /device:TPU:1, one launch (start us, length us, event | category | flops | bytes accessed | tf_op | source)
XLA Modules:
  0.0 437.2 jit_solution(15637913423461812515)
XLA Ops:
  7.2 0.0 all-gather.3.cloned.1.call-start
  7.2 2.2 bitcast_convert_fusion
  9.4 0.0 all-gather.3.cloned.1.call-update
  9.4 0.0 reduce-scatter.3.cloned.1.call-start
  9.5 0.7 dynamic-slice_select_fusion
  10.2 0.1 select_n.68
  10.3 0.7 dynamic-slice_select_fusion.1
  11.1 0.1 select_n.66
  11.2 0.7 fusion.18
  12.0 0.1 fusion.14
  12.1 0.7 iota_reduce_fusion.1
  12.8 11.5 %compare_select_fusion.1 = (s32[288]{0:T(512)S(1)}, s32[288]{0:T(512)S(1)}) fusion(s32[288]{0:T(512)S(1)} %get-tuple-element.6, s32[]{:T(128)} %bitcast.21, s32[]{:T(128)} %bitcast.20, s32[]{:T(128)} %bitcast.19, s32[]{:T(128)} %bitcast.18, s32[]{:T(128)} %bitcast.17, s32[]{:T(128)} %bitcast.16, s32[]{:T(128)} %bitcast.15, s32[]{:T(128)} %bitcast.14, ...), kind=kLoop, calls=%fused_computation.29 | loop fusion | flops 10656 | bytes 3528 | tf_op jit(solution)/shard_map/jit(_take)/jit(_where)/select_n | solution.py:29
  24.2 0.3 fusion.13
  24.6 1.4 fusion.19
  25.9 10.3 %gather_fusion = bf16[288,128,128]{2,1,0:T(8,128)(2,1)} fusion(bf16[18,128,128]{2,1,0:T(8,128)(2,1)S(1)} %fusion.19, s32[1024]{0:T(1024)S(1)} %pad_clamp_fusion.1), kind=kCustom, calls=%fused_computation.clone | custom fusion | bytes 18875520 | tf_op jit(solution)/shard_map/jit(_take)/gather | solution.py:29
  36.3 0.9 iota_reduce_fusion
  37.2 93.4 %all-gather.3.cloned.1.call-done = bf16[1,1,288,128,128]{4,3,1,0,2:T(8,128)(2,1)} async-done(((bf16[1,1,18,128,128]{4,3,1,0,2:T(8,128)(2,1)}), bf16[1,1,288,128,128]{4,3,1,0,2:T(8,128)(2,1)}) %all-gather.3.cloned.1.call-update) | async-done | bytes 9437200 | tf_op jit(solution)/shard_map/all_gather | solution.py:50
  130.6 13.6 %gather_fusion.1 = bf16[288,128,128]{2,1,0:T(8,128)(2,1)} fusion(bf16[288,128,128]{2,1,0:T(8,128)(2,1)} %bitcast.45, s32[1024]{0:T(1024)S(1)} %pad_clamp_fusion), kind=kCustom, calls=%fused_computation.1.clone | custom fusion | bytes 18875520 | tf_op jit(solution)/shard_map/jit(_take)/gather | solution.py:30
  144.3 13.4 %multiply_convert_fusion.1 = bf16[288,128,128]{2,1,0:T(8,128)(2,1)} fusion(f32[288]{0:T(512)S(1)} %convert_element_type.37, bf16[288,128,128]{2,1,0:T(8,128)(2,1)} %gather_fusion, pred[288]{0:T(512)(128)(4,1)S(1)} %compare_and_fusion.2, bf16[288,128,128]{2,1,0:T(8,128)(2,1)} %gather_fusion.1, pred[288]{0:T(512)(128)(4,1)S(1)} %compare_and_fusion.1), kind=kOutput, calls=%fused_computation.4 | convolution fusion | flops 1226833920 | bytes 28313280 | tf_op jit(solution)/shard_map/nik,njk->nij/dot_general | solution.py:31
  157.7 0.0 reduce-scatter.3.cloned.1.call-update
  157.7 0.2 reduce-scatter.5.cloned.1.call-start
  157.9 85.9 %reduce-scatter.3.cloned.1.call-done = bf16[18,128,128]{2,1,0:T(8,128)(2,1)} async-done(((bf16[288,128,128]{2,1,0:T(8,128)(2,1)}), bf16[18,128,128]{2,1,0:T(8,128)(2,1)}) %reduce-scatter.3.cloned.1.call-update) | async-done | bytes 589840 | tf_op jit(solution)/shard_map/reduce_scatter | solution.py:32
  243.8 11.4 %gather_fusion.2 = bf16[288,128,128]{2,1,0:T(8,128)(2,1)} fusion(bf16[18,128,128]{2,1,0:T(8,128)(2,1)} %reduce-scatter.3.cloned.1.call-done, s32[1024]{0:T(1024)S(1)} %pad_clamp_fusion.1), kind=kCustom, calls=%fused_computation.2.clone | custom fusion | bytes 18875520 | tf_op jit(solution)/shard_map/jit(_take)/gather | solution.py:29
  255.2 13.4 %multiply_convert_fusion = bf16[288,128,128]{2,1,0:T(8,128)(2,1)} fusion(f32[288]{0:T(512)S(1)} %convert_element_type.37, bf16[288,128,128]{2,1,0:T(8,128)(2,1)} %gather_fusion.2, pred[288]{0:T(512)(128)(4,1)S(1)} %compare_and_fusion.2, bf16[288,128,128]{2,1,0:T(8,128)(2,1)} %gather_fusion.1, pred[288]{0:T(512)(128)(4,1)S(1)} %compare_and_fusion.1), kind=kOutput, calls=%fused_computation.3 | convolution fusion | flops 1226833920 | bytes 28313280 | tf_op jit(solution)/shard_map/nik,njk->nij/dot_general | solution.py:31
  268.6 0.0 copy-start
  268.6 0.0 reduce-scatter.5.cloned.1.call-update
  268.6 78.3 %reduce-scatter.5.cloned.1.call-done = bf16[18,128,128]{2,1,0:T(8,128)(2,1)} async-done(((bf16[288,128,128]{2,1,0:T(8,128)(2,1)}), bf16[18,128,128]{2,1,0:T(8,128)(2,1)}) %reduce-scatter.5.cloned.1.call-update) | async-done | bytes 589840 | tf_op jit(solution)/shard_map/reduce_scatter | solution.py:32
  347.0 0.0 copy-done
  347.0 2.4 select_reduce_fusion
  349.3 0.6 fusion.15
  349.9 79.0 %psum.7 = f32[]{:T(128)} all-reduce(f32[]{:T(128)} %fusion.15), channel_id=1, replica_groups=mesh['row'=16,'col'=16] {'row','col'}, use_global_device_ids=true, to_apply=%region_8.11 | all-reduce | flops 1 | bytes 8 | tf_op jit(solution)/shard_map/psum | solution.py:58
  (13 shorter events, 0.1 us)
Async XLA Ops:
  7.2 123.5 %all-gather.3.cloned.1.call-start = ((), (), s32[]{:S(2)}) async-start(), calls=%async_computation.4 | async-start | bytes 10027008 | tf_op jit(solution)/shard_map/all_gather | solution.py:50
  9.4 234.4 %reduce-scatter.3.cloned.1.call-start = ((), (), s32[]{:S(2)}) async-start(), calls=%async_computation.2 | async-start | bytes 10027008 | tf_op jit(solution)/shard_map/reduce_scatter | solution.py:32
  157.7 189.3 %reduce-scatter.5.cloned.1.call-start = ((), (), s32[]{:S(2)}) async-start(), calls=%async_computation.3 | async-start | bytes 10027008 | tf_op jit(solution)/shard_map/reduce_scatter | solution.py:32
  268.6 78.4 %copy-start = (bf16[18,128,128]{2,1,0:T(8,128)(2,1)S(1)}, bf16[18,128,128]{2,1,0:T(8,128)(2,1)}, u32[]{:S(2)}) copy-start(bf16[18,128,128]{2,1,0:T(8,128)(2,1)} %reduce-scatter.3.cloned.1.call-done) | copy-start | bytes 1769476
Sparse Core Ops, SparseCore 0:
  11.0 119.5 all-gather.2
  157.8 85.9 reduce-scatter.2
  268.7 78.1 reduce-scatter.4
where the time goes:
time: 438 us; the launch traced here: 437 us
  waiting for transfers between devices  258 us (59%)
  blocking collectives  79 us (18%)
  local copies, waits for them, and re-layouts  36.3 us (8%)
  matrix products  26.8 us (6%)
  other arithmetic  21.6 us (5%)
  between operations  15.6 us (4%)
    reduce_scatter x2, waiting for transfers between devices, scattered_product(): lax.psum_scatter((result * weight[:, None, None]).astype(jnp.bfloat16), '...  164 us
    all_gather x1, waiting for transfers between devices, per_device(): mirror = lax.all_gather(own_low, 'row', axis=0, tiled=True)  93.4 us
    psum x1, blocking collectives, per_device(): lax.psum(jnp.sum(jnp.where(own_diag, jnp.einsum('nii->n', purified), 0.0)...  79 us
    dot_general x2, matrix products, scattered_product(): jnp.einsum('nik,njk->nij', left_rows, right_rows, preferred_element_type=...  26.8 us
    gather x2, local copies, waits for them, and re-layouts, scattered_product(): left_rows = jnp.take(left, left_slot, axis=0)  21.7 us
    gather x1, local copies, waits for them, and re-layouts, scattered_product(): right_rows = jnp.take(mirror, right_slot, axis=0)  13.6 us
    select_n x1, other arithmetic, scattered_product(): left_rows = jnp.take(left, left_slot, axis=0)  11.5 us
  transfers between devices with their start and end apart: 3, of which 3 were waited for; matrix products, arithmetic and copies ran while one was open for 6% of the time, Pallas kernels for 0%

commit v1 on v0

v1 whole, which is shorter than its diff:
```python
import jax
import jax.numpy as jnp
from jax import lax
from jax.experimental import pallas as pl
from jax.experimental.pallas import tpu as pltpu
from jax.sharding import PartitionSpec as P

NB = 512
BLK = 128
TILES = 18
PACK = BLK + 16
BF = jnp.bfloat16
F32 = jnp.float32
MESH = pl.DeviceIdType.MESH

CHIP_STEPS = ((0, 1), (0, 3), (1, 0), (0, 2), (1, 1), (1, 3), (1, 2))
RING_STEPS = (1, 3, 2)

SRC, DIDX, EIDX, DIAG, TABLE = 0, 32, 64, 96, 128


def dot(a, b):
    return jnp.dot(a, b, preferred_element_type=F32)


def dot_t(a, b):
    return lax.dot_general(a, b, (((1,), (1,)), ((), ())), preferred_element_type=F32)


def grids():
    row = lax.broadcasted_iota(jnp.int32, (BLK, BLK), 0)
    col = lax.broadcasted_iota(jnp.int32, (BLK, BLK), 1)
    return row, col


def pack(first, second):
    row, col = grids()
    body = jnp.where(row <= col, first, second)
    diag = jnp.sum(jnp.where(row == col, second, 0.0), axis=0, keepdims=True)
    return body, jnp.broadcast_to(diag, (PACK - BLK, BLK))


def unpack(body, diag):
    row, col = grids()
    turned = body.T
    first = jnp.where(row <= col, body, turned)
    second = jnp.where(row > col, body, jnp.where(row < col, turned, diag))
    return first, second


def kernel(
    table, dens_hbm, out_hbm, special, trace,
    dens, tiles, terms, dpack, epack, spack, mine, twins, summed, landed, sums,
    dfull, efull, sfull, square, outs, tcol, trow,
    load_sem, d_send, d_recv, e_send, e_recv, s_send, s_recv,
    x_send, x_recv, r_send, r_recv, tc_send, tc_recv, tr_send, tr_recv, out_sem,
):
    me_r = lax.axis_index("row")
    me_c = lax.axis_index("col")
    core = lax.rem(me_c, 2)
    other = 1 - core
    chip = me_c // 2
    zlo, y = chip // 4, lax.rem(chip, 4)
    zhi, x = me_r // 4, lax.rem(me_r, 4)
    twin = chip * 2 + other
    chips = [lax.rem(zlo + dz, 2) * 4 + lax.rem(y + dy, 4) for dz, dy in CHIP_STEPS]
    zs = [lax.rem(zhi + d, 4) for d in RING_STEPS]
    xs = [lax.rem(x + d, 4) for d in RING_STEPS]

    barrier = pltpu.get_barrier_semaphore()
    load = pltpu.make_async_copy(dens_hbm, dens, load_sem)
    load.start()

    @pl.loop(1, 16)
    def _(i):
        pl.semaphore_signal(barrier, inc=1, device_id={"col": lax.rem(me_c + i, 16)}, device_id_type=MESH)
        pl.semaphore_signal(barrier, inc=1, device_id={"row": lax.rem(me_r + i, 16)}, device_id_type=MESH)

    def to_col(src, dst, send, recv, c):
        return pltpu.make_async_remote_copy(
            src_ref=src, dst_ref=dst, send_sem=send, recv_sem=recv,
            device_id={"col": c}, device_id_type=MESH,
        )

    def to_row(src, dst, send, recv, r):
        return pltpu.make_async_remote_copy(
            src_ref=src, dst_ref=dst, send_sem=send, recv_sem=recv,
            device_id={"row": r}, device_id_type=MESH,
        )

    def spread_start(buf, send, recv):
        own = buf.at[core, chip]
        for n, ch in enumerate(chips):
            to_col(own, own, send.at[n], recv.at[core, chip], ch * 2 + core).start()
        to_col(own, own, send.at[7], recv.at[core, chip], twin).start()

    def spread_forward(buf, send, recv, n):
        part = buf.at[core, chips[n]]
        copy = to_col(part, part, send.at[8 + n], recv.at[core, chips[n]], twin)
        copy.wait_recv()
        copy.start()

    def spread_twin(buf, send, recv, ch):
        part = buf.at[other, ch]
        to_col(part, part, send.at[0], recv.at[other, ch], twin).wait_recv()

    def spread_end(buf, send, recv):
        own = buf.at[core, chip]
        for n in range(15):
            to_col(own, own, send.at[n], recv.at[core, chip], twin).wait_send()

    def reduce_pack(skip_own, which):
        @pl.loop(0, 8)
        def _(k):
            i0 = table[SRC + (which * 8 + k) * 2]
            i1 = table[SRC + (which * 8 + k) * 2 + 1]
            if skip_own:
                own = jnp.logical_and(which == core, k == chip)
                i0 = jnp.where(own, TILES, i0)
                i1 = jnp.where(own, TILES, i1)
            body, diag = pack(terms[i0].astype(F32), terms[i1].astype(F32))
            mine[which, k, 0:BLK] = body.astype(BF)
            mine[which, k, BLK:PACK] = diag.astype(BF)

    def twin_copy(s):
        return to_col(mine.at[other], twins.at[s], x_send.at[s], x_recv.at[s], twin)

    def reduce_send(s):
        twin_copy(s).wait_recv()

        @pl.loop(0, 8)
        def _(k):
            summed[s, k] = (mine[core, k].astype(F32) + twins[s, k].astype(F32)).astype(BF)

        for n, ch in enumerate(chips):
            to_col(summed.at[s, ch], landed.at[s, chip], r_send.at[s, n], r_recv.at[s, chip], ch * 2 + core).start()

    def reduce_end(s):
        total = summed[s, chip].astype(F32)
        for n, ch in enumerate(chips):
            to_col(summed.at[s, ch], landed.at[s, ch], r_send.at[s, n], r_recv.at[s, ch], ch * 2 + core).wait_recv()
            total = total + landed[s, ch].astype(F32)
        sums[s] = total

    load.wait()

    @pl.loop(0, TILES)
    def _(t):
        tiles[t] = dens[t].astype(BF)

    zero = jnp.zeros((BLK, BLK), BF)
    tiles[TILES] = zero
    terms[TILES] = zero
    my_pos = (core * 8 + chip) * 2
    own0 = table[SRC + my_pos]
    own1 = table[SRC + my_pos + 1]
    body, diag = pack(tiles[own0].astype(F32), tiles[own1].astype(F32))
    body, diag = body.astype(BF), diag.astype(BF)
    dpack[core, chip, 0:BLK] = body
    dpack[core, chip, BLK:PACK] = diag
    epack[zhi, x, 0:BLK] = body
    epack[zhi, x, BLK:PACK] = diag

    pl.semaphore_wait(barrier, 30)

    def along_z(n):
        own = epack.at[zhi, x]
        return to_row(own, own, e_send.at[n], e_recv.at[zhi, x], zs[n] * 4 + x)

    def along_x(z, m, n):
        part = epack.at[z, x]
        return to_row(part, part, e_send.at[m], e_recv.at[z, x], zhi * 4 + xs[n])

    for n in range(3):
        along_z(n).start()
    for n in range(3):
        along_x(zhi, 3 + n, n).start()
    spread_start(dpack, d_send, d_recv)

    @pl.loop(0, TILES)
    def _(t):
        b = tiles[t]
        terms[t] = dot_t(b, b).astype(BF)

    reduce_pack(False, other)
    twin_copy(0).start()
    reduce_pack(False, core)

    for n in range(3):
        part = epack.at[zs[n], x]
        to_row(part, part, e_send.at[0], e_recv.at[zs[n], x], me_r).wait_recv()
        for m in range(3):
            along_x(zs[n], 6 + 3 * n + m, m).start()

    reduce_send(0)

    def expand(buf, which, k, full, at):
        first, second = unpack(buf[which, k, 0:BLK].astype(F32), buf[which, k, BLK:BLK + 1].astype(F32))
        full[at] = first.astype(BF)
        full[at + 1] = second.astype(BF)

    for n in range(7):
        spread_forward(dpack, d_send, d_recv, n)

    @pl.loop(0, 8)
    def _(k):
        expand(dpack, core, k, dfull, (core * 8 + k) * 2)

    reduce_end(0)
    total = sums[0]
    spack[core, chip] = total.astype(BF)
    spread_start(spack, s_send, s_recv)

    for ch in range(8):
        spread_twin(dpack, d_send, d_recv, ch)

    @pl.loop(0, 8)
    def _(k):
        expand(dpack, other, k, dfull, (other * 8 + k) * 2)

    @pl.loop(0, TILES)
    def _(t):
        square[t] = dot(dfull[table[DIDX + t]], tiles[t])

    for n in range(3):
        part = epack.at[zhi, xs[n]]
        to_row(part, part, e_send.at[0], e_recv.at[zhi, xs[n]], me_r).wait_recv()
    for m in range(3):
        for n in range(3):
            part = epack.at[zs[m], xs[n]]
            to_row(part, part, e_send.at[0], e_recv.at[zs[m], xs[n]], me_r).wait_recv()

    @pl.loop(0, 4)
    def _(z):
        for k in range(4):
            expand(epack, z, k, efull, (z * 4 + k) * 2)

    twin_copy(0).wait_send()

    @pl.loop(0, TILES)
    def _(t):
        b = tiles[t]
        f = dot(b, efull[table[EIDX + t]])
        square[t] = square[t] + f
        terms[t] = dot_t(f.astype(BF), b).astype(BF)

    reduce_pack(True, other)
    twin_copy(1).start()
    reduce_pack(True, core)

    def fold(v):
        return jnp.sum(v.reshape(BLK // 8, 8, BLK), axis=0)

    def step(t, acc):
        b = tiles[t]
        s = square[t]
        low = s.astype(BF)
        outs[t] = 3.0 * s - 2.0 * dot(low, efull[table[EIDX + t]])
        wide = b.astype(F32)
        off = (1 - table[DIAG + t]).astype(F32)
        return acc + fold(wide * (3.0 * wide - (2.0 * off) * low.astype(F32)))

    acc = lax.fori_loop(0, TILES, step, jnp.zeros((8, BLK), F32))

    s0, s1 = unpack(sums[0, 0:BLK], sums[0, BLK:BLK + 1])
    for h, s in ((0, s0), (1, s1)):
        d = tiles[own0 if h == 0 else own1]
        low = s.astype(BF)
        rest = (s - dot(d, d)).astype(BF)
        special[h] = 3.0 * s - 2.0 * (dot(d, rest) + dot(low, d))
        acc = acc - 2.0 * fold(low.astype(F32) * d.astype(F32))
    tcol[me_c] = acc

    reduce_send(1)

    @pl.loop(1, 16)
    def _(i):
        to_col(tcol.at[me_c], tcol.at[me_c], tc_send.at[i], tc_recv.at[me_c], lax.rem(me_c + i, 16)).start()

    for n in range(7):
        spread_forward(spack, s_send, s_recv, n)

    @pl.loop(0, 8)
    def _(k):
        expand(spack, core, k, sfull, (core * 8 + k) * 2)

    for ch in range(8):
        spread_twin(spack, s_send, s_recv, ch)

    @pl.loop(0, 8)
    def _(k):
        expand(spack, other, k, sfull, (other * 8 + k) * 2)

    @pl.loop(1, 16)
    def _(i):
        c = lax.rem(me_c + i, 16)
        to_col(tcol.at[c], tcol.at[c], tc_send.at[i], tc_recv.at[c], c).wait_recv()

    trow[me_r] = jnp.sum(tcol[...], axis=0)

    @pl.loop(1, 16)
    def _(i):
        to_row(trow.at[me_r], trow.at[me_r], tr_send.at[i], tr_recv.at[me_r], lax.rem(me_r + i, 16)).start()

    @pl.loop(0, TILES)
    def _(t):
        outs[t] = outs[t] - 2.0 * dot(sfull[table[DIDX + t]], tiles[t])

    store = pltpu.make_async_copy(outs, out_hbm, out_sem)
    store.start()

    reduce_end(1)
    q0, q1 = unpack(sums[1, 0:BLK], sums[1, BLK:BLK + 1])
    special[0] = special[0] - 2.0 * q0
    special[1] = special[1] - 2.0 * q1

    @pl.loop(1, 16)
    def _(i):
        r = lax.rem(me_r + i, 16)
        to_row(trow.at[r], trow.at[r], tr_send.at[i], tr_recv.at[r], r).wait_recv()

    trace[0, 0] = jnp.sum(trow[...]) / (NB * BLK)

    spread_end(dpack, d_send, d_recv)
    spread_end(spack, s_send, s_recv)
    own = epack.at[zhi, x]
    for n in range(15):
        to_row(own, own, e_send.at[n], e_recv.at[zhi, x], me_r).wait_send()
    twin_copy(1).wait_send()
    for s in range(2):
        for n, ch in enumerate(chips):
            to_col(summed.at[s, ch], landed.at[s, ch], r_send.at[s, n], r_recv.at[s, ch], ch * 2 + core).wait_send()

    @pl.loop(1, 16)
    def _(i):
        to_col(tcol.at[me_c], tcol.at[me_c], tc_send.at[i], tc_recv.at[me_c], lax.rem(me_c + i, 16)).wait_send()
        to_row(trow.at[me_r], trow.at[me_r], tr_send.at[i], tr_recv.at[me_r], lax.rem(me_r + i, 16)).wait_send()

    store.wait()


def fast_call(table, dens):
    dma = pltpu.SemaphoreType.DMA
    return pl.pallas_call(
        kernel,
        out_shape=(
            jax.ShapeDtypeStruct((TILES, BLK, BLK), F32),
            jax.ShapeDtypeStruct((2, BLK, BLK), F32),
            jax.ShapeDtypeStruct((1, 1), F32),
        ),
        in_specs=[pl.BlockSpec(memory_space=pltpu.SMEM), pl.BlockSpec(memory_space=pl.ANY)],
        out_specs=(
            pl.BlockSpec(memory_space=pl.ANY),
            pl.BlockSpec(memory_space=pltpu.VMEM),
            pl.BlockSpec(memory_space=pltpu.SMEM),
        ),
        scratch_shapes=[
            pltpu.VMEM((TILES, BLK, BLK), F32),
            pltpu.VMEM((TILES + 1, BLK, BLK), BF),
            pltpu.VMEM((TILES + 1, BLK, BLK), BF),
            pltpu.VMEM((2, 8, PACK, BLK), BF),
            pltpu.VMEM((4, 4, PACK, BLK), BF),
            pltpu.VMEM((2, 8, PACK, BLK), BF),
            pltpu.VMEM((2, 8, PACK, BLK), BF),
            pltpu.VMEM((2, 8, PACK, BLK), BF),
            pltpu.VMEM((2, 8, PACK, BLK), BF),
            pltpu.VMEM((2, 8, PACK, BLK), BF),
            pltpu.VMEM((2, PACK, BLK), F32),
            pltpu.VMEM((32, BLK, BLK), BF),
            pltpu.VMEM((32, BLK, BLK), BF),
            pltpu.VMEM((32, BLK, BLK), BF),
            pltpu.VMEM((TILES, BLK, BLK), F32),
            pltpu.VMEM((TILES, BLK, BLK), F32),
            pltpu.VMEM((16, 8, BLK), F32),
            pltpu.VMEM((16, 8, BLK), F32),
            dma(()),
            dma((15,)), dma((2, 8)),
            dma((15,)), dma((4, 4)),
            dma((15,)), dma((2, 8)),
            dma((2,)), dma((2,)),
            dma((2, 7)), dma((2, 8)),
            dma((16,)), dma((16,)),
            dma((16,)), dma((16,)),
            dma(()),
        ],
        compiler_params=pltpu.CompilerParams(
            collective_id=0, has_side_effects=True, vmem_limit_bytes=40 * 1024 * 1024
        ),
    )(table, dens)


def index_table(own, tile_coords):
    rows, cols = own[:, 0], own[:, 1]
    column_class = (tile_coords[0, :, 0, 1] & 15).reshape(8, 2).T.reshape(16)
    match = (rows[:, None] & 15) == column_class[None, :]
    half = rows >> 8
    place = jnp.sum(jnp.where(match, jnp.arange(16, dtype=jnp.int32)[None, :], 0), axis=1)
    slots = jnp.arange(TILES, dtype=jnp.int32) - TILES
    hit = match[:, :, None] & (half[:, None, None] == jnp.arange(2, dtype=jnp.int32)[None, None, :])
    src = jnp.sum(jnp.where(hit, slots[:, None, None], 0), axis=0).reshape(32) + TILES
    band = cols >> 4
    gap = jnp.zeros((14,), jnp.int32)
    return jnp.concatenate([
        src,
        place * 2 + half, gap,
        (band & 15) * 2 + (band >> 4), gap,
        (rows == cols).astype(jnp.int32), gap,
    ])


def fast(density, tile_coords, own):
    out, special, trace = fast_call(index_table(own, tile_coords), density[0, 0])
    on_diag = own[:, 0] == own[:, 1]
    high = own[:, 0] >= NB // 2
    out = jnp.where(
        on_diag[:, None, None], jnp.where(high[:, None, None], special[1][None], special[0][None]), out
    )
    return out[None, None], trace[0, 0]


def pair_lookup(own_coords, targets, mirror_coords):
    own_rows = own_coords[:, 0]
    own_cols = own_coords[:, 1]
    target_row = targets[:, 0]
    target_col = targets[:, 1]
    first = (own_rows[None, :] == target_row[:, None]) & (target_row[:, None] >= 0)
    has_first = jnp.any(first, axis=1)
    left_slot = jnp.argmax(first.astype(jnp.int32), axis=1)
    inner = own_cols[left_slot]
    second = (mirror_coords[None, :, 0] == target_col[:, None]) & (
        mirror_coords[None, :, 1] == inner[:, None]
    )
    second = second & has_first[:, None]
    keep = jnp.any(second, axis=1)
    right_slot = jnp.argmax(second.astype(jnp.int32), axis=1)
    return (left_slot, right_slot, keep)


def scattered_product(left, mirror, left_slot, right_slot, keep):
    weight = keep.astype(F32)
    left_rows = jnp.take(left, left_slot, axis=0)
    right_rows = jnp.take(mirror, right_slot, axis=0)
    result = jnp.einsum("nik,njk->nij", left_rows, right_rows, preferred_element_type=F32)
    return lax.psum_scatter(
        (result * weight[:, None, None]).astype(BF), "col", scatter_dimension=0, tiled=True
    ).astype(F32)


def general(density, tile_coords, own_coords):
    own_tiles = density[0, 0]
    own_low = own_tiles.astype(BF)
    my_row = lax.axis_index("row")
    my_col = lax.axis_index("col")
    row_flat = jnp.take(tile_coords, my_row, axis=0).reshape(-1, 2)
    col_flat = jnp.take(tile_coords, my_col, axis=1).reshape(-1, 2)
    mirror = lax.all_gather(own_low, "row", axis=0, tiled=True)
    own_diag = own_coords[:, 0] == own_coords[:, 1]
    left_slot, right_slot, keep = pair_lookup(own_coords, row_flat, col_flat)
    square = scattered_product(own_low, mirror, left_slot, right_slot, keep)
    square_low = square.astype(BF)
    cube = scattered_product(square_low, mirror, left_slot, right_slot, keep)
    purified = 3.0 * square - 2.0 * cube
    total = lax.psum(
        jnp.sum(jnp.where(own_diag, jnp.einsum("nii->n", purified), 0.0)), ("row", "col")
    )
    return purified[None, None], total / (NB * BLK)


def per_device(density, tile_coords):
    own = lax.dynamic_slice(
        tile_coords, (lax.axis_index("row"), lax.axis_index("col"), 0, 0), (1, 1, TILES, 2)
    )[0, 0]
    offsets = (own[:, 1] - own[:, 0]) & (NB - 1)
    sums = (offsets[:, None] + offsets[None, :]) & (NB - 1)
    live = (offsets[:, None] != 0) & (offsets[None, :] != 0)
    triple = live[:, :, None] & (offsets != 0) & (sums[:, :, None] == offsets)
    return lax.cond(jnp.any(triple), general, fast, density, tile_coords, own)


def solution(mesh):
    return jax.shard_map(
        per_device,
        mesh=mesh,
        in_specs=(P("row", "col", None, None, None), P()),
        out_specs=(P("row", "col", None, None, None), P()),
        check_vma=False,
    )
```

time: 438 us -> 71 us (0.16)
  waiting for transfers between devices: 258 us -> 0 us
  blocking collectives: 79 us -> 0 us
  Pallas kernels: 0 us -> 49.7 us
  local copies, waits for them, and re-layouts: 36.3 us -> 2.76 us
  matrix products: 26.8 us -> 0 us
  other arithmetic: 21.6 us -> 1.58 us
    reduce_scatter x2 -> x0, waiting for transfers between devices: 164 us -> none  [scattered_product(): lax.psum_scatter((result * weight[:, None, None]).astype(jnp.bfloat16), '...]
    all_gather x1 -> x0, waiting for transfers between devices: 93.4 us -> none  [per_device(): mirror = lax.all_gather(own_low, 'row', axis=0, tiled=True)]
    psum x1 -> x0, blocking collectives: 79 us -> none  [per_device(): lax.psum(jnp.sum(jnp.where(own_diag, jnp.einsum('nii->n', purified), 0.0)...]
    pallas_call x0 -> x1, Pallas kernels: none -> 49.7 us  [fast_call(): pl.pallas_call(kernel, out_shape=(jax.ShapeDtypeStruct((TILES, BLK, BLK),...]
    gather x4 -> x0, local copies, waits for them, and re-layouts: 36.1 us -> none  [the longest x2 21.7 us: scattered_product(): left_rows = jnp.take(left, left_slot, axis=0)]
    dot_general x2 -> x0, matrix products: 26.8 us -> none  [scattered_product(): jnp.einsum('nik,njk->nij', left_rows, right_rows, preferred_element_type=...]
    select_n x5 -> x0, other arithmetic: 13 us -> none  [the longest x1 11.5 us: scattered_product(): left_rows = jnp.take(left, left_slot, axis=0)]
  transfers between devices with their start and end apart: 3 -> 0, of which waited for: 3 -> 0; matrix products, arithmetic and copies ran while one was open for 6% -> 0% of each run, Pallas kernels for 0% -> 0%
where the time goes in v1:
time: 71 us; the launch traced here: 70.8 us
  Pallas kernels  49.7 us (70%)
  between operations  16.5 us (23%)
  local copies, waits for them, and re-layouts  2.76 us (4%)
  other arithmetic  1.58 us (2%)
    pallas_call x1, Pallas kernels, fast_call(): pl.pallas_call(kernel, out_shape=(jax.ShapeDtypeStruct((TILES, BLK, BLK),...  49.7 us

profile of v1, /device:TPU:1, one launch (start us, length us, event | category | flops | bytes accessed | tf_op | source)
XLA Modules:
  0.0 70.8 jit_solution(10900724554095595933)
XLA Ops:
  7.2 0.7 dynamic-slice_bitcast_fusion
  7.9 0.1 broadcast_and_fusion
  7.9 0.1 add_and_fusion
  8.0 0.8 %and_reduce_fusion = pred[]{:T(512)} fusion(s32[18]{0:T(128)S(1)} %bitcast.73, s32[18,18]{1,0:T(8,128)S(1)} %add_and_fusion, pred[18]{0:T(512)(128)(4,1)S(1)} %broadcast_compare_fusion.1, pred[18,18]{1,0:T(8,128)(4,1)S(1)} %broadcast_and_fusion), kind=kLoop, calls=%fused_computation.61 | loop fusion | flops 23327 | bytes 1711 | tf_op jit(solution)/shard_map/reduce_or | solution.py:477
  9.5 52.4 %conditional.1 = (f32[1,1,18,128,128]{4,3,2,1,0:T(8,128)S(1)}, f32[]{:T(128)}) conditional(s32[]{:T(128)} %convert_element_type.39, (s32[18,2]{0,1:T(2,128)S(1)}, s32[16,16,18,2]{2,3,1,0:T(2,128)}, f32[1,1,18,128,128]{4,3,2,1,0:T(8,128)}) %tuple.21, (f32[1,1,18,128,128]{4,3,2,1,0:T(8,128)}, s32[18,2]{0,1:T(2,128)S(1)}, ...), branch_computations={%region_1.4_spmd, %region_4.16_spmd} | conditional | flops 2457829888 | bytes 211933472 | solution.py:477
  9.5 1.2 %copy.22 = s32[16,16,18,2]{1,3,2,0:T(2,128)S(1)} copy(s32[16,16,18,2]{2,3,1,0:T(2,128)} %get-tuple-element.67) | data formatting | bytes 73728 | tf_op jit(solution)/shard_map
  10.8 0.1 and.113
  10.9 0.1 copy.19
  10.9 0.1 eq.65
  11.0 0.1 broadcast_compare_fusion
  11.1 0.1 select_reduce_fusion.1
  11.3 0.1 copy.20
  11.4 0.1 add.56
  11.4 0.1 select_reduce_fusion.2
  11.6 0.1 concatenate.2.table
  11.7 49.7 %branch_0_fun.1 = (f32[18,128,128]{2,1,0:T(8,128)S(1)}, f32[2,128,128]{2,1,0:T(8,128)S(1)}, f32[1,1]{1,0:T(1,128)}) custom-call(s32[128]{0:T(128)S(1)} %concatenate.2.table, f32[18,128,128]{2,1,0:T(8,128)} %bitcast.69), custom_call_target="tpu_custom_call" | custom-call | tf_op jit(solution)/shard_map/cond/branch_0_fun/pallas_call | solution.py:344
  61.3 0.2 select_bitcast_fusion
  61.9 0.0 copy-start.1
  62.6 0.3 copy-done.1
  (11 shorter events, 0.1 us)
Async XLA Ops:
  61.9 1.0 %copy-start.1 = (f32[1,1,18,128,128]{4,3,2,1,0:T(8,128)}, f32[1,1,18,128,128]{4,3,2,1,0:T(8,128)S(1)}, u32[]{:S(2)}) copy-start(f32[1,1,18,128,128]{4,3,2,1,0:T(8,128)S(1)} %get-tuple-element.116) | copy-start | bytes 3538948

commit v2 on v1

v2 whole, which is shorter than its diff:
```python
import jax
import jax.numpy as jnp
from jax import lax
from jax.experimental import pallas as pl
from jax.experimental.pallas import tpu as pltpu
from jax.sharding import PartitionSpec as P

NB = 512
BLK = 128
TILES = 18
PACK = BLK + 16
BF = jnp.bfloat16
F32 = jnp.float32
MESH = pl.DeviceIdType.MESH

CHIP_STEPS = ((0, 1), (0, 3), (1, 0), (0, 2), (1, 1), (1, 3), (1, 2))
RING_STEPS = (1, 3, 2)

SRC, DIDX, EIDX, KEY, TABLE = 0, 32, 64, 96, 128


def dot(a, b):
    return jnp.dot(a, b, preferred_element_type=F32)


def dot_t(a, b):
    return lax.dot_general(a, b, (((1,), (1,)), ((), ())), preferred_element_type=F32)


def each(n):
    return pl.loop(0, n, unroll=True)


def grids():
    row = lax.broadcasted_iota(jnp.int32, (BLK, BLK), 0)
    col = lax.broadcasted_iota(jnp.int32, (BLK, BLK), 1)
    return row, col


def pack(first, second):
    row, col = grids()
    body = jnp.where(row <= col, first, second)
    diag = jnp.sum(jnp.where(row == col, second, 0.0), axis=0, keepdims=True)
    return body, jnp.broadcast_to(diag, (PACK - BLK, BLK))


def unpack(body, diag):
    row, col = grids()
    turned = body.T
    first = jnp.where(row <= col, body, turned)
    second = jnp.where(row > col, body, jnp.where(row < col, turned, diag))
    return first, second


def fill_table(coords, table, me_c):
    def column_class(place):
        return coords[lax.rem(place, 8) * 2 + place // 8, 1, 0] & 15

    classes = [column_class(place) for place in range(16)]
    keys = []
    for t in range(TILES):
        i, j = coords[me_c, 0, t], coords[me_c, 1, t]
        residue, half = i & 15, i >> 8
        place = jnp.int32(0)
        for n in range(16):
            place = jnp.where(classes[n] == residue, n, place)
        table[DIDX + t] = place * 2 + half
        table[EIDX + t] = ((j >> 4) & 15) * 2 + (j >> 8)
        keys.append(place * 2 + half)
    for n in range(32):
        slot = jnp.int32(TILES)
        for t in range(TILES):
            slot = jnp.where(keys[t] == n, t, slot)
        table[SRC + n] = slot


def any_triple(coords, lanes, me_c):
    wide = (lanes[1:2] - lanes[0:1]) & (NB - 1)
    wide = jnp.where(wide == 0, -2, wide)
    offsets = [(coords[me_c, 1, t] - coords[me_c, 0, t]) & (NB - 1) for t in range(TILES)]
    found = jnp.zeros(wide.shape, jnp.int32)
    for s in range(TILES):
        for t in range(s, TILES):
            live = jnp.logical_and(offsets[s] != 0, offsets[t] != 0)
            both = jnp.where(live, (offsets[s] + offsets[t]) & (NB - 1), -1)
            found = found | (wide == both).astype(jnp.int32)
    return jnp.max(found)


def kernel(
    coords_hbm, dens_hbm, out_hbm, special, trace, flag,
    coords, table, lanes, dens, tiles, terms, dpack, epack, spack, mine, twins, summed, landed, sums,
    dfull, efull, sfull, square, outs, tcol, trow,
    load_sem, coord_sem, d_send, d_recv, e_send, e_recv, s_send, s_recv,
    x_send, x_recv, r_send, r_recv, tc_send, tc_recv, tr_send, tr_recv, out_sem,
):
    me_r = lax.axis_index("row")
    me_c = lax.axis_index("col")
    core = lax.rem(me_c, 2)
    other = 1 - core
    chip = me_c // 2
    zlo, y = chip // 4, lax.rem(chip, 4)
    zhi, x = me_r // 4, lax.rem(me_r, 4)
    twin = chip * 2 + other
    chips = [lax.rem(zlo + dz, 2) * 4 + lax.rem(y + dy, 4) for dz, dy in CHIP_STEPS]
    zs = [lax.rem(zhi + d, 4) for d in RING_STEPS]
    xs = [lax.rem(x + d, 4) for d in RING_STEPS]

    barrier = pltpu.get_barrier_semaphore()
    get_coords = pltpu.make_async_copy(coords_hbm.at[me_r], coords, coord_sem.at[0])
    get_lanes = pltpu.make_async_copy(coords_hbm.at[me_r, me_c], lanes, coord_sem.at[1])
    load = pltpu.make_async_copy(dens_hbm, dens, load_sem)
    get_coords.start()
    load.start()
    get_lanes.start()

    for i in range(1, 16):
        pl.semaphore_signal(barrier, inc=1, device_id={"row": lax.rem(me_r + i, 16)}, device_id_type=MESH)
    for i in range(1, 16):
        pl.semaphore_signal(barrier, inc=1, device_id={"col": lax.rem(me_c + i, 16)}, device_id_type=MESH)

    def to_col(src, dst, send, recv, c):
        return pltpu.make_async_remote_copy(
            src_ref=src, dst_ref=dst, send_sem=send, recv_sem=recv,
            device_id={"col": c}, device_id_type=MESH,
        )

    def to_row(src, dst, send, recv, r):
        return pltpu.make_async_remote_copy(
            src_ref=src, dst_ref=dst, send_sem=send, recv_sem=recv,
            device_id={"row": r}, device_id_type=MESH,
        )

    def spread_start(buf, send, recv):
        own = buf.at[core, chip]
        for n, ch in enumerate(chips):
            to_col(own, own, send.at[n], recv.at[core, chip], ch * 2 + core).start()
        to_col(own, own, send.at[7], recv.at[core, chip], twin).start()

    def spread_forward(buf, send, recv):
        for n, ch in enumerate(chips):
            part = buf.at[core, ch]
            copy = to_col(part, part, send.at[8 + n], recv.at[core, ch], twin)
            copy.wait_recv()
            copy.start()

    def spread_twin(buf, send, recv):
        for ch in [chip] + chips:
            part = buf.at[other, ch]
            to_col(part, part, send.at[0], recv.at[other, ch], twin).wait_recv()

    def spread_end(buf, send, recv):
        own = buf.at[core, chip]
        for n in range(15):
            to_col(own, own, send.at[n], recv.at[core, chip], twin).wait_send()

    def reduce_pack(skip_own, which):
        @each(8)
        def _(k):
            i0 = table[SRC + (which * 8 + k) * 2]
            i1 = table[SRC + (which * 8 + k) * 2 + 1]
            if skip_own:
                own = jnp.logical_and(which == core, k == chip)
                i0 = jnp.where(own, TILES, i0)
                i1 = jnp.where(own, TILES, i1)
            body, diag = pack(terms[i0].astype(F32), terms[i1].astype(F32))
            mine[which, k, 0:BLK] = body.astype(BF)
            mine[which, k, BLK:PACK] = diag.astype(BF)

    def twin_copy(s):
        return to_col(mine.at[other], twins.at[s], x_send.at[s], x_recv.at[s], twin)

    def reduce_send(s):
        twin_copy(s).wait_recv()

        @each(8)
        def _(k):
            summed[s, k] = (mine[core, k].astype(F32) + twins[s, k].astype(F32)).astype(BF)

        for n, ch in enumerate(chips):
            to_col(summed.at[s, ch], landed.at[s, chip], r_send.at[s, n], r_recv.at[s, chip], ch * 2 + core).start()

    def reduce_end(s):
        total = summed[s, chip].astype(F32)
        for n, ch in enumerate(chips):
            to_col(summed.at[s, ch], landed.at[s, ch], r_send.at[s, n], r_recv.at[s, ch], ch * 2 + core).wait_recv()
            total = total + landed[s, ch].astype(F32)
        sums[s] = total

    def expand(buf, which, k, full, at):
        first, second = unpack(buf[which, k, 0:BLK].astype(F32), buf[which, k, BLK:BLK + 1].astype(F32))
        full[at] = first.astype(BF)
        full[at + 1] = second.astype(BF)

    def expand_half(buf, which, full):
        @each(8)
        def _(k):
            expand(buf, which, k, full, (which * 8 + k) * 2)

    def fold(v):
        return jnp.sum(v.reshape(BLK // 8, 8, BLK), axis=0)

    get_coords.wait()
    fill_table(coords, table, me_c)
    load.wait()

    @each(TILES)
    def _(t):
        tiles[t] = dens[t].astype(BF)

    zero = jnp.zeros((BLK, BLK), BF)
    tiles[TILES] = zero
    terms[TILES] = zero
    my_pos = (core * 8 + chip) * 2
    own0 = table[SRC + my_pos]
    own1 = table[SRC + my_pos + 1]
    body, diag = pack(tiles[own0].astype(F32), tiles[own1].astype(F32))
    body, diag = body.astype(BF), diag.astype(BF)
    dpack[core, chip, 0:BLK] = body
    dpack[core, chip, BLK:PACK] = diag
    epack[zhi, x, 0:BLK] = body
    epack[zhi, x, BLK:PACK] = diag

    @each(TILES)
    def _(t):
        b = tiles[t]
        terms[t] = dot_t(b, b).astype(BF)

    reduce_pack(False, other)

    pl.semaphore_wait(barrier, 30)

    def along_z(n):
        own = epack.at[zhi, x]
        return to_row(own, own, e_send.at[n], e_recv.at[zhi, x], zs[n] * 4 + x)

    def along_x(z, m, n):
        part = epack.at[z, x]
        return to_row(part, part, e_send.at[m], e_recv.at[z, x], zhi * 4 + xs[n])

    def arrived(z, k):
        part = epack.at[z, k]
        to_row(part, part, e_send.at[0], e_recv.at[z, k], me_r).wait_recv()

    for n in range(3):
        along_z(n).start()
    twin_copy(0).start()
    for n in range(3):
        along_x(zhi, 3 + n, n).start()
    reduce_pack(False, core)
    reduce_send(0)
    spread_start(dpack, d_send, d_recv)

    for n in range(3):
        arrived(zs[n], x)
        for m in range(3):
            along_x(zs[n], 6 + 3 * n + m, m).start()

    get_lanes.wait()
    flag[0, 0] = any_triple(coords, lanes, me_c)
    spread_forward(dpack, d_send, d_recv)

    reduce_end(0)
    spack[core, chip] = sums[0].astype(BF)
    spread_start(spack, s_send, s_recv)

    acc = jnp.zeros((8, BLK), F32)
    row, col = grids()
    for h, s in enumerate(unpack(sums[0, 0:BLK], sums[0, BLK:BLK + 1])):
        d = tiles[own0 if h == 0 else own1]
        wide = d.astype(F32)
        low = s.astype(BF)
        rest = s - dot(d, d)
        special[h] = 3.0 * s - 2.0 * (dot(d, rest.astype(BF)) + dot(low, d))
        acc = acc + fold(jnp.where(row == col, 3.0 * s, 0.0) - wide * (4.0 * rest + 2.0 * s))
    tcol[me_c] = acc
    for i in range(1, 16):
        to_col(tcol.at[me_c], tcol.at[me_c], tc_send.at[i], tc_recv.at[me_c], lax.rem(me_c + i, 16)).start()

    expand_half(dpack, core, dfull)
    spread_twin(dpack, d_send, d_recv)
    expand_half(dpack, other, dfull)

    @each(TILES)
    def _(t):
        square[t] = dot(dfull[table[DIDX + t]], tiles[t])

    for n in range(3):
        arrived(zhi, xs[n])
    for m in range(3):
        for n in range(3):
            arrived(zs[m], xs[n])

    @each(16)
    def _(k):
        expand(epack, k // 4, lax.rem(k, 4), efull, k * 2)

    twin_copy(0).wait_send()

    @each(TILES)
    def _(t):
        b = tiles[t]
        f = dot(b, efull[table[EIDX + t]])
        square[t] = square[t] + f
        terms[t] = dot_t(f.astype(BF), b).astype(BF)

    reduce_pack(True, other)
    twin_copy(1).start()
    reduce_pack(True, core)

    for i in range(1, 16):
        c = lax.rem(me_c + i, 16)
        to_col(tcol.at[c], tcol.at[c], tc_send.at[i], tc_recv.at[c], c).wait_recv()
    trow[me_r] = jnp.sum(tcol[...], axis=0)
    for i in range(1, 16):
        to_row(trow.at[me_r], trow.at[me_r], tr_send.at[i], tr_recv.at[me_r], lax.rem(me_r + i, 16)).start()

    reduce_send(1)
    spread_forward(spack, s_send, s_recv)

    @each(TILES)
    def _(t):
        s = square[t]
        outs[t] = 3.0 * s - 2.0 * dot(s.astype(BF), efull[table[EIDX + t]])

    expand_half(spack, core, sfull)
    spread_twin(spack, s_send, s_recv)
    expand_half(spack, other, sfull)

    @each(TILES)
    def _(t):
        outs[t] = outs[t] - 2.0 * dot(sfull[table[DIDX + t]], tiles[t])

    store = pltpu.make_async_copy(outs, out_hbm, out_sem)
    store.start()

    reduce_end(1)
    for h, q in enumerate(unpack(sums[1, 0:BLK], sums[1, BLK:BLK + 1])):
        special[h] = special[h] - 2.0 * q

    for i in range(1, 16):
        r = lax.rem(me_r + i, 16)
        to_row(trow.at[r], trow.at[r], tr_send.at[i], tr_recv.at[r], r).wait_recv()
    trace[0, 0] = jnp.sum(trow[...]) / (NB * BLK)

    spread_end(dpack, d_send, d_recv)
    spread_end(spack, s_send, s_recv)
    own = epack.at[zhi, x]
    for n in range(15):
        to_row(own, own, e_send.at[n], e_recv.at[zhi, x], me_r).wait_send()
    twin_copy(1).wait_send()
    for s in range(2):
        for n, ch in enumerate(chips):
            to_col(summed.at[s, ch], landed.at[s, ch], r_send.at[s, n], r_recv.at[s, ch], ch * 2 + core).wait_send()
    for i in range(1, 16):
        to_col(tcol.at[me_c], tcol.at[me_c], tc_send.at[i], tc_recv.at[me_c], lax.rem(me_c + i, 16)).wait_send()
        to_row(trow.at[me_r], trow.at[me_r], tr_send.at[i], tr_recv.at[me_r], lax.rem(me_r + i, 16)).wait_send()
    store.wait()


def fast_call(coords, dens):
    dma = pltpu.SemaphoreType.DMA
    pair = (2, 8, PACK, BLK)
    return pl.pallas_call(
        kernel,
        out_shape=(
            jax.ShapeDtypeStruct((TILES, BLK, BLK), F32),
            jax.ShapeDtypeStruct((2, BLK, BLK), F32),
            jax.ShapeDtypeStruct((1, 1), F32),
            jax.ShapeDtypeStruct((1, 1), jnp.int32),
        ),
        in_specs=[pl.BlockSpec(memory_space=pl.ANY), pl.BlockSpec(memory_space=pl.ANY)],
        out_specs=(
            pl.BlockSpec(memory_space=pl.ANY),
            pl.BlockSpec(memory_space=pltpu.VMEM),
            pl.BlockSpec(memory_space=pltpu.SMEM),
            pl.BlockSpec(memory_space=pltpu.SMEM),
        ),
        scratch_shapes=[
            pltpu.SMEM((16, 2, TILES), jnp.int32),
            pltpu.SMEM((TABLE,), jnp.int32),
            pltpu.VMEM((2, TILES), jnp.int32),
            pltpu.VMEM((TILES, BLK, BLK), F32),
            pltpu.VMEM((TILES + 1, BLK, BLK), BF),
            pltpu.VMEM((TILES + 1, BLK, BLK), BF),
            pltpu.VMEM(pair, BF),
            pltpu.VMEM((4, 4, PACK, BLK), BF),
            pltpu.VMEM(pair, BF),
            pltpu.VMEM(pair, BF),
            pltpu.VMEM(pair, BF),
            pltpu.VMEM(pair, BF),
            pltpu.VMEM(pair, BF),
            pltpu.VMEM((2, PACK, BLK), F32),
            pltpu.VMEM((32, BLK, BLK), BF),
            pltpu.VMEM((32, BLK, BLK), BF),
            pltpu.VMEM((32, BLK, BLK), BF),
            pltpu.VMEM((TILES, BLK, BLK), F32),
            pltpu.VMEM((TILES, BLK, BLK), F32),
            pltpu.VMEM((16, 8, BLK), F32),
            pltpu.VMEM((16, 8, BLK), F32),
            dma(()), dma((2,)),
            dma((15,)), dma((2, 8)),
            dma((15,)), dma((4, 4)),
            dma((15,)), dma((2, 8)),
            dma((2,)), dma((2,)),
            dma((2, 7)), dma((2, 8)),
            dma((16,)), dma((16,)),
            dma((16,)), dma((16,)),
            dma(()),
        ],
        compiler_params=pltpu.CompilerParams(
            collective_id=0, has_side_effects=True, vmem_limit_bytes=40 * 1024 * 1024
        ),
    )(coords, dens)


def pair_lookup(own_coords, targets, mirror_coords):
    own_rows = own_coords[:, 0]
    own_cols = own_coords[:, 1]
    target_row = targets[:, 0]
    target_col = targets[:, 1]
    first = own_rows[None, :] == target_row[:, None]
    has_first = jnp.any(first, axis=1)
    left_slot = jnp.argmax(first.astype(jnp.int32), axis=1)
    inner = own_cols[left_slot]
    second = (mirror_coords[None, :, 0] == target_col[:, None]) & (
        mirror_coords[None, :, 1] == inner[:, None]
    )
    second = second & has_first[:, None]
    keep = jnp.any(second, axis=1)
    right_slot = jnp.argmax(second.astype(jnp.int32), axis=1)
    return (left_slot, right_slot, keep)


def to_all(value, axis):
    return lax.all_to_all(jnp.broadcast_to(value[None], (16,) + value.shape), axis, 0, 0)


def scattered_product(left, mirror, left_slot, right_slot, keep):
    weight = keep.astype(F32)
    left_rows = jnp.take(left, left_slot, axis=0)
    right_rows = jnp.take(mirror, right_slot, axis=0)
    result = jnp.einsum("nik,njk->nij", left_rows, right_rows, preferred_element_type=F32)
    result = (result * weight[:, None, None]).astype(BF).reshape(16, TILES, BLK, BLK)
    return jnp.sum(lax.all_to_all(result, "col", 0, 0).astype(F32), axis=0)


def general(density, tile_coords):
    own_tiles = density[0, 0]
    own_low = own_tiles.astype(BF)
    my_row = lax.axis_index("row")
    my_col = lax.axis_index("col")
    row_table = jnp.take(tile_coords, my_row, axis=0)
    own_coords = jnp.take(row_table, my_col, axis=0)
    row_flat = row_table.reshape(-1, 2)
    col_flat = jnp.take(tile_coords, my_col, axis=1).reshape(-1, 2)
    mirror = to_all(own_low, "row").reshape(-1, BLK, BLK)
    own_diag = own_coords[:, 0] == own_coords[:, 1]
    left_slot, right_slot, keep = pair_lookup(own_coords, row_flat, col_flat)
    square = scattered_product(own_low, mirror, left_slot, right_slot, keep)
    square_low = square.astype(BF)
    cube = scattered_product(square_low, mirror, left_slot, right_slot, keep)
    purified = 3.0 * square - 2.0 * cube
    total = jnp.sum(jnp.where(own_diag, jnp.einsum("nii->n", purified), 0.0))
    total = jnp.sum(to_all(jnp.sum(to_all(total, "col")), "row"))
    return purified, total / (NB * BLK)


def per_device(density, tile_coords):
    out, special, trace, flag = fast_call(tile_coords.transpose(0, 1, 3, 2), density[0, 0])
    own = lax.dynamic_slice(
        tile_coords, (lax.axis_index("row"), lax.axis_index("col"), 0, 0), (1, 1, TILES, 2)
    )[0, 0]
    on_diag = own[:, 0] == own[:, 1]
    high = own[:, 0] >= NB // 2
    out = jnp.where(
        on_diag[:, None, None], jnp.where(high[:, None, None], special[1][None], special[0][None]), out
    )
    out, mean_diagonal = lax.cond(
        flag[0, 0] > 0,
        lambda out, trace: general(density, tile_coords),
        lambda out, trace: (out, trace),
        out, trace[0, 0],
    )
    return out[None, None], mean_diagonal


def solution(mesh):
    return jax.shard_map(
        per_device,
        mesh=mesh,
        in_specs=(P("row", "col", None, None, None), P()),
        out_specs=(P("row", "col", None, None, None), P()),
        check_vma=False,
    )
```

time: 71 us -> 45.8 us (0.65)
  between operations: 16.5 us -> 3.1 us
  Pallas kernels: 49.7 us -> 40.5 us
  local copies, waits for them, and re-layouts: 2.76 us -> 0.7 us
    pallas_call x1, Pallas kernels: 49.7 us -> 40.5 us  [fast_call(): pl.pallas_call(kernel, out_shape=(jax.ShapeDtypeStruct((TILES, BLK, BLK),...]
    another operation x2 -> x0, local copies, waits for them, and re-layouts: 1.24 us -> none
    broadcast_in_dim x1, other arithmetic: 0.25 us -> 1.26 us  [per_device(): return (out[None, None], mean_diagonal)]
    reduce_or x1 -> x0, other arithmetic: 0.82 us -> none  [per_device(): return lax.cond(jnp.any(triple), general, fast, density, tile_coords, own)]
where the time goes in v2:
time: 45.8 us; the launch traced here: 45.6 us
  Pallas kernels  40.5 us (88%)
  between operations  3.1 us (7%)
  other arithmetic  1.27 us (3%)
  local copies, waits for them, and re-layouts  0.7 us (2%)
    pallas_call x1, Pallas kernels, fast_call(): pl.pallas_call(kernel, out_shape=(jax.ShapeDtypeStruct((TILES, BLK, BLK),...  40.5 us
    broadcast_in_dim x1, other arithmetic, per_device(): return (out[None, None], mean_diagonal)  1.26 us

profile of v2, /device:TPU:1, one launch (start us, length us, event | category | flops | bytes accessed | tf_op | source)
XLA Modules:
  0.0 45.6 jit_solution(10154015573390763584)
XLA Ops:
  0.6 40.5 %shard_map.41 = (f32[18,128,128]{2,1,0:T(8,128)S(1)}, f32[2,128,128]{2,1,0:T(8,128)S(1)}, f32[1,1]{1,0:T(1,128)}, s32[1,1]{1,0:T(1,128)}) custom-call(s32[16,16,2,18]{3,2,1,0:T(2,128)} %bitcast.59, f32[18,128,128]{2,1,0:T(8,128)} %bitcast.58), custom_call_target="tpu_custom_call" | custom-call | tf_op jit(solution)/shard_map/pallas_call | solution.py:364
  41.9 2.0 %conditional.1 = (f32[]{:T(128)}, f32[1,1,18,128,128]{4,3,2,1,0:T(8,128)}) conditional(s32[]{:T(128)} %bitcast.35, (f32[1,1]{1,0:T(1,128)}, s32[]{:T(128)}, s32[]{:T(128)}, s32[16,16,18,2]{2,3,1,0:T(2,128)}, f32[2,128,128]{2,1,0:T(8,128)S(1)}, /*index=5*/f32[18,128,128]{2,1,0:T(8,128)S(1)}) %tuple.75, (s32[16,16,18,2]{2,3,1,0:T(2,128)}, ...), branch_computations={%region_0.1_spmd, %region_1.14_spmd} | conditional | flops 2475514112 | bytes 227415104 | solution.py:479
  41.9 0.7 %dynamic-slice_bitcast_fusion = s32[18,2]{0,1:T(2,128)S(1)} fusion(s32[16,16,18,2]{2,3,1,0:T(2,128)} %get-tuple-element.63, s32[]{:T(128)S(6)} %select_n.62, s32[]{:T(128)S(6)} %select_n.63), kind=kLoop, calls=%fused_computation.8 | loop fusion | bytes 296 | tf_op jit(solution)/shard_map/squeeze | solution.py:471
  42.6 1.3 %select_bitcast_fusion = f32[1,1,18,128,128]{4,3,2,1,0:T(8,128)} fusion(f32[18,128,128]{2,1,0:T(8,128)S(1)} %get-tuple-element.67, f32[128,128]{1,0:T(8,128)S(1)} %get-tuple-element.130, f32[128,128]{1,0:T(8,128)S(1)} %get-tuple-element.129, pred[18]{0:T(512)(128)(4,1)S(1)} %get-tuple-element.132, pred[18]{0:T(512)(128)(4,1)S(1)} %get-tuple-element.131), kind=kLoop, calls=%fused_computation.3 | loop fusion | flops 589824 | bytes 2490404 | tf_op jit(solution)/shard_map/broadcast_in_dim | solution.py:485
  (2 shorter events, 0.0 us)

commit v3 on v2

v3 whole, which is shorter than its diff:
```python
import jax
import jax.numpy as jnp
from jax import lax
from jax.experimental import pallas as pl
from jax.experimental.pallas import tpu as pltpu
from jax.sharding import PartitionSpec as P

NB = 512
BLK = 128
TILES = 18
PACK = BLK + 16
BF = jnp.bfloat16
F32 = jnp.float32
MESH = pl.DeviceIdType.MESH

CHIP_STEPS = ((0, 0), (0, 1), (0, 3), (1, 0), (0, 2), (1, 1), (1, 3), (1, 2))
CHIP_BACK = tuple(CHIP_STEPS.index((-dz % 2, -dy % 4)) for dz, dy in CHIP_STEPS)
RING = (0, 1, 3, 2)
RING_BACK = tuple(RING.index(-d % 4) for d in RING)

SRC, DIDX, EIDX, TABLE = 0, 32, 64, 96


def dot(a, b):
    return jnp.dot(a, b, preferred_element_type=F32)


def dot_t(a, b):
    return lax.dot_general(a, b, (((1,), (1,)), ((), ())), preferred_element_type=F32)


def each(lo, hi):
    return pl.loop(lo, hi, unroll=True)


def grids():
    row = lax.broadcasted_iota(jnp.int32, (BLK, BLK), 0)
    col = lax.broadcasted_iota(jnp.int32, (BLK, BLK), 1)
    return row, col


def pack(first, second):
    row, col = grids()
    body = jnp.where(row <= col, first, second)
    diag = jnp.sum(jnp.where(row == col, second, 0.0), axis=0, keepdims=True)
    return body, jnp.broadcast_to(diag, (PACK - BLK, BLK))


def unpack(body, diag):
    row, col = grids()
    turned = body.T
    first = jnp.where(row <= col, body, turned)
    second = jnp.where(row > col, body, jnp.where(row < col, turned, diag))
    return first, second


def fill_table(coords, table, which, me_r, me_c, places):
    classes = [coords[c, 1, 0] & 15 for c in places]
    zhi, x = me_r // 4, lax.rem(me_r, 4)
    keys = []
    for t in range(TILES):
        i, j = coords[me_c, 0, t], coords[me_c, 1, t]
        residue, half = i & 15, i >> 8
        place = jnp.int32(0)
        for n in range(16):
            place = jnp.where(classes[n] == residue, n, place)
        key = place * 2 + half
        keys.append(key)
        table[DIDX + t] = key
        dz, dx = ((j >> 6) - zhi) & 3, ((j >> 4) - x) & 3
        table[EIDX + t] = ((dx ^ (dx >> 1)) * 4 + (dz ^ (dz >> 1))) * 2 + (j >> 8)
        which[t] = jnp.where(i == j, 1 + half, 0)
    for n in range(32):
        slot = jnp.int32(TILES)
        for t in range(TILES):
            slot = jnp.where(keys[t] == n, t, slot)
        table[SRC + n] = slot


def diagonal_slots(coords, me_c):
    first, second = jnp.int32(0), jnp.int32(0)
    for t in range(TILES):
        i, j = coords[me_c, 0, t], coords[me_c, 1, t]
        first = jnp.where(jnp.logical_and(i == j, i < NB // 2), t, first)
        second = jnp.where(jnp.logical_and(i == j, i >= NB // 2), t, second)
    return first, second


def any_triple(coords, lanes, me_c):
    wide = (lanes[1:2] - lanes[0:1]) & (NB - 1)
    wide = jnp.where(wide == 0, -2, wide)
    offsets = [(coords[me_c, 1, t] - coords[me_c, 0, t]) & (NB - 1) for t in range(TILES)]
    found = jnp.zeros(wide.shape, jnp.int32)
    for s in range(TILES):
        for t in range(s, TILES):
            live = jnp.logical_and(offsets[s] != 0, offsets[t] != 0)
            both = jnp.where(live, (offsets[s] + offsets[t]) & (NB - 1), -1)
            found = found | (wide == both).astype(jnp.int32)
    return jnp.max(found)


def kernel(
    coords_hbm, dens_hbm, out_hbm, special, trace, flag, which,
    coords, table, lanes, dens, tiles, terms, dpack, epack, spack, mine, twins, summed, landed, sums,
    dfull, efull, sfull, square, outs, ttwin, tcol, tz, tx,
    load_sem, d_send, d_recv, e_send, ez_recv, ex_recv, s_send, s_recv,
    x_send, x_recv, r_send, r_recv, t_send, t_recv, out_sem,
):
    me_r = lax.axis_index("row")
    me_c = lax.axis_index("col")
    core = lax.rem(me_c, 2)
    chip = me_c // 2
    zlo, y = chip // 4, lax.rem(chip, 4)
    zhi, x = me_r // 4, lax.rem(me_r, 4)
    chips = [lax.rem(zlo + dz, 2) * 4 + lax.rem(y + dy, 4) for dz, dy in CHIP_STEPS]
    same = [ch * 2 + core for ch in chips]
    places = same + [ch * 2 + 1 - core for ch in chips]
    twin = places[8]
    zs = [lax.rem(zhi + d, 4) * 4 + x for d in RING]
    xs = [zhi * 4 + lax.rem(x + d, 4) for d in RING]

    barrier = pltpu.get_barrier_semaphore()
    get_coords = pltpu.make_async_copy(coords_hbm.at[me_r], coords, load_sem.at[0])
    load = pltpu.make_async_copy(dens_hbm, dens, load_sem.at[1])
    get_lanes = pltpu.make_async_copy(coords_hbm.at[me_r, me_c], lanes, load_sem.at[2])
    get_coords.start()
    load.start()
    for b in (3, 2, 1):
        pl.semaphore_signal(barrier, inc=1, device_id={"row": zs[b]}, device_id_type=MESH)
    for k in range(7, 0, -1):
        pl.semaphore_signal(barrier, inc=1, device_id={"col": same[k]}, device_id_type=MESH)
    for a in (3, 2, 1):
        pl.semaphore_signal(barrier, inc=1, device_id={"row": xs[a]}, device_id_type=MESH)
    pl.semaphore_signal(barrier, inc=1, device_id={"col": twin}, device_id_type=MESH)
    get_lanes.start()

    def to_col(src, dst, send, recv, c):
        return pltpu.make_async_remote_copy(
            src_ref=src, dst_ref=dst, send_sem=send, recv_sem=recv,
            device_id={"col": c}, device_id_type=MESH,
        )

    def to_row(src, dst, send, recv, r):
        return pltpu.make_async_remote_copy(
            src_ref=src, dst_ref=dst, send_sem=send, recv_sem=recv,
            device_id={"row": r}, device_id_type=MESH,
        )

    def spread_start(buf, send, recv):
        for k in range(1, 8):
            to_col(buf.at[0, 0], buf.at[0, CHIP_BACK[k]], send.at[0], recv.at[0], same[k]).start()

    def spread_seven(buf, send, recv):
        part = buf.at[0, 1:8]
        return to_col(part, part, send.at[0], recv.at[0], twin)

    def spread_twin(buf, send, recv):
        return to_col(buf.at[0], buf.at[1], send.at[1], recv.at[1], twin)

    def reduce_pack(rc, first):
        @each(first, 8)
        def _(k):
            n = rc * 8 + k
            body, diag = pack(terms[table[SRC + n * 2]].astype(F32), terms[table[SRC + n * 2 + 1]].astype(F32))
            mine[rc, k, 0:BLK] = body.astype(BF)
            mine[rc, k, BLK:PACK] = diag.astype(BF)

    def twin_copy(s):
        return to_col(mine.at[1], twins.at[s], x_send.at[s], x_recv.at[s], twin)

    def reduce_send(s):
        twin_copy(s).wait_recv()
        for k in range(7, -1, -1):
            summed[s, k] = (mine[0, k].astype(F32) + twins[s, k].astype(F32)).astype(BF)
            if k:
                to_col(summed.at[s, k], landed.at[s, CHIP_BACK[k]], r_send.at[s], r_recv.at[s], same[k]).start()

    def reduce_seven(s):
        return to_col(summed.at[s, 1:8], landed.at[s, 1:8], r_send.at[s], r_recv.at[s], twin)

    def reduce_end(s):
        reduce_seven(s).wait_recv()
        total = summed[s, 0].astype(F32)
        for k in range(1, 8):
            total = total + landed[s, k].astype(F32)
        sums[s] = total

    def expand(buf, n, m, full, at):
        first, second = unpack(buf[n, m, 0:BLK].astype(F32), buf[n, m, BLK:BLK + 1].astype(F32))
        full[at] = first.astype(BF)
        full[at + 1] = second.astype(BF)

    def expand_half(buf, rc, full):
        @each(0, 8)
        def _(k):
            expand(buf, rc, k, full, (rc * 8 + k) * 2)

    def fold(v):
        return jnp.sum(v.reshape(BLK // 8, 8, BLK), axis=0)

    get_coords.wait()
    own0, own1 = diagonal_slots(coords, me_c)
    load.wait()

    @each(0, TILES)
    def _(t):
        tiles[t] = dens[t].astype(BF)

    zero = jnp.zeros((BLK, BLK), BF)
    tiles[TILES] = zero
    terms[TILES] = zero
    body, diag = pack(tiles[own0].astype(F32), tiles[own1].astype(F32))
    body, diag = body.astype(BF), diag.astype(BF)
    dpack[0, 0, 0:BLK] = body
    dpack[0, 0, BLK:PACK] = diag
    epack[0, 0, 0:BLK] = body
    epack[0, 0, BLK:PACK] = diag

    pl.semaphore_wait(barrier, 14)
    for b in (3, 1, 2):
        to_row(epack.at[0, 0], epack.at[0, RING_BACK[b]], e_send.at[0], ez_recv.at[b // 3], zs[b]).start()

    def along_x(lo, hi, n):
        for a in (3, 1, 2):
            to_row(
                epack.at[0, lo:hi], epack.at[RING_BACK[a], lo:hi], e_send.at[1 + n], ex_recv.at[n], xs[a]
            ).start()

    def ring_wait(part, sem):
        return to_row(part, part, e_send.at[0], sem, me_r)

    along_x(0, 1, 0)

    fill_table(coords, table, which, me_r, me_c, places)

    @each(0, TILES)
    def _(t):
        b = tiles[t]
        terms[t] = dot_t(b, b).astype(BF)

    reduce_pack(1, 0)
    twin_copy(0).start()
    reduce_pack(0, 0)

    ring_wait(epack.at[0, 1:3], ez_recv.at[0]).wait_recv()
    along_x(1, 3, 0)
    reduce_send(0)
    ring_wait(epack.at[0, 3], ez_recv.at[1]).wait_recv()
    along_x(3, 4, 1)
    spread_start(dpack, d_send, d_recv)

    get_lanes.wait()
    flag[0, 0] = any_triple(coords, lanes, me_c)

    reduce_end(0)
    spack[0, 0] = sums[0].astype(BF)
    spread_start(spack, s_send, s_recv)

    acc = jnp.zeros((8, BLK), F32)
    row, col = grids()
    for h, s in enumerate(unpack(sums[0, 0:BLK], sums[0, BLK:BLK + 1])):
        d = tiles[own0 if h == 0 else own1]
        wide = d.astype(F32)
        low = s.astype(BF)
        rest = s - dot(d, d)
        special[h] = 3.0 * s - 2.0 * (dot(d, rest.astype(BF)) + dot(low, d))
        acc = acc + fold(jnp.where(row == col, 3.0 * s, 0.0) - wide * (4.0 * rest + 2.0 * s))
    ttwin[0] = acc
    trace_twin = to_col(ttwin.at[0], ttwin.at[1], t_send.at[0], t_recv.at[0], twin)
    trace_twin.start()

    spread_seven(dpack, d_send, d_recv).wait_recv()
    spread_twin(dpack, d_send, d_recv).start()
    expand_half(dpack, 0, dfull)

    trace_twin.wait_recv()
    tcol[0] = ttwin[0] + ttwin[1]
    for k in range(1, 8):
        to_col(tcol.at[0], tcol.at[CHIP_BACK[k]], t_send.at[1], t_recv.at[1], same[k]).start()

    spread_twin(dpack, d_send, d_recv).wait_recv()
    expand_half(dpack, 1, dfull)

    @each(0, TILES)
    def _(t):
        square[t] = dot(dfull[table[DIDX + t]], tiles[t])

    for b in range(4):
        expand(epack, 0, b, efull, b * 2)
    ring_wait(epack.at[1:4, 0:3], ex_recv.at[0]).wait_recv()
    for a in range(1, 4):
        for b in range(3):
            expand(epack, a, b, efull, (a * 4 + b) * 2)
    twin_copy(0).wait_send()
    ring_wait(epack.at[1:4, 3], ex_recv.at[1]).wait_recv()
    for a in range(1, 4):
        expand(epack, a, 3, efull, (a * 4 + 3) * 2)

    @each(0, TILES)
    def _(t):
        b = tiles[t]
        f = dot(b, efull[table[EIDX + t]])
        square[t] = square[t] + f
        terms[t] = dot_t(f.astype(BF), b).astype(BF)

    reduce_pack(1, 0)
    twin_copy(1).start()
    reduce_pack(0, 1)
    mine[0, 0] = jnp.zeros((PACK, BLK), BF)

    tcol_seven = to_col(tcol.at[1:8], tcol.at[1:8], t_send.at[1], t_recv.at[1], twin)
    tcol_seven.wait_recv()
    tz[0] = jnp.sum(tcol[...], axis=0)
    for b in (3, 1, 2):
        to_row(tz.at[0], tz.at[RING_BACK[b]], t_send.at[2], t_recv.at[2], zs[b]).start()

    reduce_send(1)

    @each(0, TILES)
    def _(t):
        s = square[t]
        outs[t] = 3.0 * s - 2.0 * dot(s.astype(BF), efull[table[EIDX + t]])

    spread_seven(spack, s_send, s_recv).wait_recv()
    spread_twin(spack, s_send, s_recv).start()
    expand_half(spack, 0, sfull)
    spread_twin(spack, s_send, s_recv).wait_recv()
    expand_half(spack, 1, sfull)

    @each(0, TILES)
    def _(t):
        outs[t] = outs[t] - 2.0 * dot(sfull[table[DIDX + t]], tiles[t])

    store = pltpu.make_async_copy(outs, out_hbm, out_sem)
    store.start()

    tz_three = to_row(tz.at[1:4], tz.at[1:4], t_send.at[2], t_recv.at[2], me_r)
    tz_three.wait_recv()
    tx[0] = jnp.sum(tz[...], axis=0)
    for a in (3, 1, 2):
        to_row(tx.at[0], tx.at[RING_BACK[a]], t_send.at[3], t_recv.at[3], xs[a]).start()

    reduce_end(1)
    for h, q in enumerate(unpack(sums[1, 0:BLK], sums[1, BLK:BLK + 1])):
        special[h] = special[h] - 2.0 * q

    for buf, send, recv in ((dpack, d_send, d_recv), (spack, s_send, s_recv)):
        spread_seven(buf, send, recv).wait_send()
        spread_twin(buf, send, recv).wait_send()
    ring_wait(epack.at[0, 1:4], ez_recv.at[0]).wait_send()
    part = epack.at[1:4, 0:3]
    to_row(part, part, e_send.at[1], ex_recv.at[0], me_r).wait_send()
    part = epack.at[1:4, 3]
    to_row(part, part, e_send.at[2], ex_recv.at[1], me_r).wait_send()
    twin_copy(1).wait_send()
    reduce_seven(0).wait_send()
    reduce_seven(1).wait_send()
    trace_twin.wait_send()
    tcol_seven.wait_send()
    tz_three.wait_send()

    tx_three = to_row(tx.at[1:4], tx.at[1:4], t_send.at[3], t_recv.at[3], me_r)
    tx_three.wait_recv()
    trace[0, 0] = jnp.sum(tx[...]) / (NB * BLK)
    tx_three.wait_send()
    store.wait()


def fast_call(coords, dens):
    dma = pltpu.SemaphoreType.DMA
    pair = (2, 8, PACK, BLK)
    smem = pl.BlockSpec(memory_space=pltpu.SMEM)
    return pl.pallas_call(
        kernel,
        out_shape=(
            jax.ShapeDtypeStruct((TILES, BLK, BLK), F32),
            jax.ShapeDtypeStruct((2, BLK, BLK), F32),
            jax.ShapeDtypeStruct((1, 1), F32),
            jax.ShapeDtypeStruct((1, 1), jnp.int32),
            jax.ShapeDtypeStruct((TILES,), jnp.int32),
        ),
        in_specs=[pl.BlockSpec(memory_space=pl.ANY), pl.BlockSpec(memory_space=pl.ANY)],
        out_specs=(
            pl.BlockSpec(memory_space=pl.ANY), pl.BlockSpec(memory_space=pltpu.VMEM), smem, smem, smem,
        ),
        scratch_shapes=[
            pltpu.SMEM((16, 2, TILES), jnp.int32),
            pltpu.SMEM((TABLE,), jnp.int32),
            pltpu.VMEM((2, TILES), jnp.int32),
            pltpu.VMEM((TILES, BLK, BLK), F32),
            pltpu.VMEM((TILES + 1, BLK, BLK), BF),
            pltpu.VMEM((TILES + 1, BLK, BLK), BF),
            pltpu.VMEM(pair, BF),
            pltpu.VMEM((4, 4, PACK, BLK), BF),
            pltpu.VMEM(pair, BF),
            pltpu.VMEM(pair, BF),
            pltpu.VMEM(pair, BF),
            pltpu.VMEM(pair, BF),
            pltpu.VMEM(pair, BF),
            pltpu.VMEM((2, PACK, BLK), F32),
            pltpu.VMEM((32, BLK, BLK), BF),
            pltpu.VMEM((32, BLK, BLK), BF),
            pltpu.VMEM((32, BLK, BLK), BF),
            pltpu.VMEM((TILES, BLK, BLK), F32),
            pltpu.VMEM((TILES, BLK, BLK), F32),
            pltpu.VMEM((2, 8, BLK), F32),
            pltpu.VMEM((8, 8, BLK), F32),
            pltpu.VMEM((4, 8, BLK), F32),
            pltpu.VMEM((4, 8, BLK), F32),
            dma((3,)),
            dma((2,)), dma((2,)),
            dma((3,)), dma((2,)), dma((2,)),
            dma((2,)), dma((2,)),
            dma((2,)), dma((2,)),
            dma((2,)), dma((2,)),
            dma((4,)), dma((4,)),
            dma(()),
        ],
        compiler_params=pltpu.CompilerParams(
            collective_id=0, has_side_effects=True, vmem_limit_bytes=40 * 1024 * 1024
        ),
    )(coords, dens)


def pair_lookup(own_coords, targets, mirror_coords):
    own_rows = own_coords[:, 0]
    own_cols = own_coords[:, 1]
    target_row = targets[:, 0]
    target_col = targets[:, 1]
    first = own_rows[None, :] == target_row[:, None]
    has_first = jnp.any(first, axis=1)
    left_slot = jnp.argmax(first.astype(jnp.int32), axis=1)
    inner = own_cols[left_slot]
    second = (mirror_coords[None, :, 0] == target_col[:, None]) & (
        mirror_coords[None, :, 1] == inner[:, None]
    )
    second = second & has_first[:, None]
    keep = jnp.any(second, axis=1)
    right_slot = jnp.argmax(second.astype(jnp.int32), axis=1)
    return (left_slot, right_slot, keep)


def to_all(value, axis):
    return lax.all_to_all(jnp.broadcast_to(value[None], (16,) + value.shape), axis, 0, 0)


def scattered_product(left, mirror, left_slot, right_slot, keep):
    weight = keep.astype(F32)
    left_rows = jnp.take(left, left_slot, axis=0)
    right_rows = jnp.take(mirror, right_slot, axis=0)
    result = jnp.einsum("nik,njk->nij", left_rows, right_rows, preferred_element_type=F32)
    result = (result * weight[:, None, None]).astype(BF).reshape(16, TILES, BLK, BLK)
    return jnp.sum(lax.all_to_all(result, "col", 0, 0).astype(F32), axis=0)


def general(density, tile_coords):
    own_tiles = density[0, 0]
    own_low = own_tiles.astype(BF)
    my_row = lax.axis_index("row")
    my_col = lax.axis_index("col")
    row_table = jnp.take(tile_coords, my_row, axis=0)
    own_coords = jnp.take(row_table, my_col, axis=0)
    row_flat = row_table.reshape(-1, 2)
    col_flat = jnp.take(tile_coords, my_col, axis=1).reshape(-1, 2)
    mirror = to_all(own_low, "row").reshape(-1, BLK, BLK)
    own_diag = own_coords[:, 0] == own_coords[:, 1]
    left_slot, right_slot, keep = pair_lookup(own_coords, row_flat, col_flat)
    square = scattered_product(own_low, mirror, left_slot, right_slot, keep)
    square_low = square.astype(BF)
    cube = scattered_product(square_low, mirror, left_slot, right_slot, keep)
    purified = 3.0 * square - 2.0 * cube
    total = jnp.sum(jnp.where(own_diag, jnp.einsum("nii->n", purified), 0.0))
    total = jnp.sum(to_all(jnp.sum(to_all(total, "col")), "row"))
    return purified, total / (NB * BLK)


def per_device(density, tile_coords):
    out, special, trace, flag, which = fast_call(tile_coords.transpose(0, 1, 3, 2), density[0, 0])
    which = which[:, None, None]
    out = jnp.where(which == 0, out, jnp.where(which == 1, special[0][None], special[1][None]))
    out, mean_diagonal = lax.cond(
        flag[0, 0] > 0,
        lambda out, trace: general(density, tile_coords),
        lambda out, trace: (out, trace),
        out, trace[0, 0],
    )
    return out[None, None], mean_diagonal


def solution(mesh):
    return jax.shard_map(
        per_device,
        mesh=mesh,
        in_specs=(P("row", "col", None, None, None), P()),
        out_specs=(P("row", "col", None, None, None), P()),
        check_vma=False,
    )
```

time: 45.8 us -> 42.3 us (0.924); the launches traced: 45.6 us -> 41.5 us
  Pallas kernels: 40.5 us -> 37.1 us
  local copies, waits for them, and re-layouts: 0.7 us -> 0.01 us
    pallas_call x1, Pallas kernels: 40.5 us -> 37.1 us  [fast_call(): pl.pallas_call(kernel, out_shape=(jax.ShapeDtypeStruct((TILES, BLK, BLK),...]
    squeeze x1 -> x0, local copies, waits for them, and re-layouts: 0.69 us -> none  [per_device(): lax.dynamic_slice(tile_coords, (lax.axis_index('row'), lax.axis_index('co...]
where the time goes in v3:
time: 42.3 us; the launch traced here: 41.5 us
  Pallas kernels  37.1 us (88%)
  between operations  3.13 us (7%)
  other arithmetic  1.27 us (3%)
    pallas_call x1, Pallas kernels, fast_call(): pl.pallas_call(kernel, out_shape=(jax.ShapeDtypeStruct((TILES, BLK, BLK),...  37.1 us
    broadcast_in_dim x1, other arithmetic, per_device(): return (out[None, None], mean_diagonal)  1.26 us

profile of v3, /device:TPU:1, one launch (start us, length us, event | category | flops | bytes accessed | tf_op | source)
XLA Modules:
  0.0 41.5 jit_solution(2981122282965107871)
XLA Ops:
  0.6 37.1 %shard_map.41 = (f32[18,128,128]{2,1,0:T(8,128)S(1)}, f32[2,128,128]{2,1,0:T(8,128)S(1)}, f32[1,1]{1,0:T(1,128)}, s32[1,1]{1,0:T(1,128)}, s32[18]{0:T(128)S(1)}) custom-call(s32[16,16,2,18]{3,2,1,0:T(2,128)} %bitcast.53, f32[18,128,128]{2,1,0:T(8,128)} %bitcast.52), custom_call_target="tpu_custom_call" | custom-call | tf_op jit(solution)/shard_map/pallas_call | solution.py:373
  38.4 1.3 %conditional.1 = (f32[]{:T(128)}, f32[1,1,18,128,128]{4,3,2,1,0:T(8,128)}) conditional(s32[]{:T(128)} %bitcast.32, (f32[1,1]{1,0:T(1,128)}, s32[18]{0:T(128)S(1)}, f32[2,128,128]{2,1,0:T(8,128)S(1)}, f32[18,128,128]{2,1,0:T(8,128)S(1)}) %tuple.73, (s32[16,16,18,2]{2,3,1,0:T(2,128)}, f32[1,1,18,128,128]{4,3,2,1,0:T(8,128)}) %tuple.26), branch_computations={%region_0.1_spmd, %region_1.14_spmd} | conditional | flops 2475514112 | bytes 227415104 | solution.py:481
  38.5 1.3 %select_bitcast_fusion = f32[1,1,18,128,128]{4,3,2,1,0:T(8,128)} fusion(f32[18,128,128]{2,1,0:T(8,128)S(1)} %get-tuple-element.38, f32[128,128]{1,0:T(8,128)S(1)} %get-tuple-element.104, f32[128,128]{1,0:T(8,128)S(1)} %get-tuple-element.103, pred[18]{0:T(512)(128)(4,1)S(1)} %get-tuple-element.106, pred[18]{0:T(512)(128)(4,1)S(1)} %get-tuple-element.105), kind=kLoop, calls=%fused_computation.3 | loop fusion | flops 589824 | bytes 2490404 | tf_op jit(solution)/shard_map/broadcast_in_dim | solution.py:487
  (2 shorter events, 0.0 us)

commit v4 on v3

--- a/solution.py
+++ b/solution.py
@@ -102,7 +102,7 @@
 def kernel(
     coords_hbm, dens_hbm, out_hbm, special, trace, flag, which,
     coords, table, lanes, dens, tiles, terms, dpack, epack, spack, mine, twins, summed, landed, sums,
-    dfull, efull, sfull, square, outs, ttwin, tcol, tz, tx,
+    dfull, efull, sfull, square, outs, tcol, tz, tx,
     load_sem, d_send, d_recv, e_send, ez_recv, ex_recv, s_send, s_recv,
     x_send, x_recv, r_send, r_recv, t_send, t_recv, out_sem,
 ):
@@ -127,11 +127,10 @@
     load.start()
     for b in (3, 2, 1):
         pl.semaphore_signal(barrier, inc=1, device_id={"row": zs[b]}, device_id_type=MESH)
-    for k in range(7, 0, -1):
-        pl.semaphore_signal(barrier, inc=1, device_id={"col": same[k]}, device_id_type=MESH)
+    for n in range(15, 0, -1):
+        pl.semaphore_signal(barrier, inc=1, device_id={"col": places[n]}, device_id_type=MESH)
     for a in (3, 2, 1):
         pl.semaphore_signal(barrier, inc=1, device_id={"row": xs[a]}, device_id_type=MESH)
-    pl.semaphore_signal(barrier, inc=1, device_id={"col": twin}, device_id_type=MESH)
     get_lanes.start()
 
     def to_col(src, dst, send, recv, c):
@@ -216,12 +215,12 @@
     epack[0, 0, 0:BLK] = body
     epack[0, 0, BLK:PACK] = diag
 
-    pl.semaphore_wait(barrier, 14)
-    for b in (3, 1, 2):
+    pl.semaphore_wait(barrier, 21)
+    for b in (1, 2, 3):
         to_row(epack.at[0, 0], epack.at[0, RING_BACK[b]], e_send.at[0], ez_recv.at[b // 3], zs[b]).start()
 
     def along_x(lo, hi, n):
-        for a in (3, 1, 2):
+        for a in (1, 2, 3):
             to_row(
                 epack.at[0, lo:hi], epack.at[RING_BACK[a], lo:hi], e_send.at[1 + n], ex_recv.at[n], xs[a]
             ).start()
@@ -245,45 +244,32 @@
     ring_wait(epack.at[0, 1:3], ez_recv.at[0]).wait_recv()
     along_x(1, 3, 0)
     reduce_send(0)
+    spread_start(dpack, d_send, d_recv)
     ring_wait(epack.at[0, 3], ez_recv.at[1]).wait_recv()
     along_x(3, 4, 1)
-    spread_start(dpack, d_send, d_recv)
 
     get_lanes.wait()
     flag[0, 0] = any_triple(coords, lanes, me_c)
 
     reduce_end(0)
     spack[0, 0] = sums[0].astype(BF)
-    spread_start(spack, s_send, s_recv)
 
     acc = jnp.zeros((8, BLK), F32)
     row, col = grids()
+    parts = []
     for h, s in enumerate(unpack(sums[0, 0:BLK], sums[0, BLK:BLK + 1])):
         d = tiles[own0 if h == 0 else own1]
-        wide = d.astype(F32)
-        low = s.astype(BF)
         rest = s - dot(d, d)
-        special[h] = 3.0 * s - 2.0 * (dot(d, rest.astype(BF)) + dot(low, d))
-        acc = acc + fold(jnp.where(row == col, 3.0 * s, 0.0) - wide * (4.0 * rest + 2.0 * s))
-    ttwin[0] = acc
-    trace_twin = to_col(ttwin.at[0], ttwin.at[1], t_send.at[0], t_recv.at[0], twin)
-    trace_twin.start()
-
-    spread_seven(dpack, d_send, d_recv).wait_recv()
-    spread_twin(dpack, d_send, d_recv).start()
-    expand_half(dpack, 0, dfull)
-
-    trace_twin.wait_recv()
-    tcol[0] = ttwin[0] + ttwin[1]
-    for k in range(1, 8):
-        to_col(tcol.at[0], tcol.at[CHIP_BACK[k]], t_send.at[1], t_recv.at[1], same[k]).start()
-
-    spread_twin(dpack, d_send, d_recv).wait_recv()
-    expand_half(dpack, 1, dfull)
-
-    @each(0, TILES)
-    def _(t):
-        square[t] = dot(dfull[table[DIDX + t]], tiles[t])
+        acc = acc + fold(jnp.where(row == col, 3.0 * s, 0.0) - d.astype(F32) * (4.0 * rest + 2.0 * s))
+        parts.append((d, s, rest))
+    tcol[0] = acc
+    for k in (8, 1, 2, 3, 9, 10, 11, 4, 5, 6, 12, 13, 14, 7, 15):
+        back = k // 8 * 8 + CHIP_BACK[k % 8]
+        to_col(tcol.at[0], tcol.at[back], t_send.at[0], t_recv.at[0], places[k]).start()
+    spread_start(spack, s_send, s_recv)
+
+    for h, (d, s, rest) in enumerate(parts):
+        special[h] = 3.0 * s - 2.0 * (dot(d, rest.astype(BF)) + dot(s.astype(BF), d))
 
     for b in range(4):
         expand(epack, 0, b, efull, b * 2)
@@ -300,7 +286,7 @@
     def _(t):
         b = tiles[t]
         f = dot(b, efull[table[EIDX + t]])
-        square[t] = square[t] + f
+        square[t] = f
         terms[t] = dot_t(f.astype(BF), b).astype(BF)
 
     reduce_pack(1, 0)
@@ -308,22 +294,36 @@
     reduce_pack(0, 1)
     mine[0, 0] = jnp.zeros((PACK, BLK), BF)
 
-    tcol_seven = to_col(tcol.at[1:8], tcol.at[1:8], t_send.at[1], t_recv.at[1], twin)
-    tcol_seven.wait_recv()
+    spread_seven(dpack, d_send, d_recv).wait_recv()
+    spread_twin(dpack, d_send, d_recv).start()
+    expand_half(dpack, 0, dfull)
+
+    reduce_send(1)
+
+    tcol_all = to_col(tcol.at[1:16], tcol.at[1:16], t_send.at[0], t_recv.at[0], twin)
+    tcol_all.wait_recv()
     tz[0] = jnp.sum(tcol[...], axis=0)
-    for b in (3, 1, 2):
-        to_row(tz.at[0], tz.at[RING_BACK[b]], t_send.at[2], t_recv.at[2], zs[b]).start()
-
-    reduce_send(1)
+    for b in (1, 2, 3):
+        to_row(tz.at[0], tz.at[RING_BACK[b]], t_send.at[1], t_recv.at[1], zs[b]).start()
+
+    spread_twin(dpack, d_send, d_recv).wait_recv()
+    expand_half(dpack, 1, dfull)
 
     @each(0, TILES)
     def _(t):
-        s = square[t]
+        s = square[t] + dot(dfull[table[DIDX + t]], tiles[t])
         outs[t] = 3.0 * s - 2.0 * dot(s.astype(BF), efull[table[EIDX + t]])
 
     spread_seven(spack, s_send, s_recv).wait_recv()
     spread_twin(spack, s_send, s_recv).start()
     expand_half(spack, 0, sfull)
+
+    tz_three = to_row(tz.at[1:4], tz.at[1:4], t_send.at[1], t_recv.at[1], me_r)
+    tz_three.wait_recv()
+    tx[0] = jnp.sum(tz[...], axis=0)
+    for a in (1, 2, 3):
+        to_row(tx.at[0], tx.at[RING_BACK[a]], t_send.at[2], t_recv.at[2], xs[a]).start()
+
     spread_twin(spack, s_send, s_recv).wait_recv()
     expand_half(spack, 1, sfull)
 
@@ -333,12 +333,6 @@
 
     store = pltpu.make_async_copy(outs, out_hbm, out_sem)
     store.start()
-
-    tz_three = to_row(tz.at[1:4], tz.at[1:4], t_send.at[2], t_recv.at[2], me_r)
-    tz_three.wait_recv()
-    tx[0] = jnp.sum(tz[...], axis=0)
-    for a in (3, 1, 2):
-        to_row(tx.at[0], tx.at[RING_BACK[a]], t_send.at[3], t_recv.at[3], xs[a]).start()
 
     reduce_end(1)
     for h, q in enumerate(unpack(sums[1, 0:BLK], sums[1, BLK:BLK + 1])):
@@ -355,11 +349,10 @@
     twin_copy(1).wait_send()
     reduce_seven(0).wait_send()
     reduce_seven(1).wait_send()
-    trace_twin.wait_send()
-    tcol_seven.wait_send()
+    tcol_all.wait_send()
     tz_three.wait_send()
 
-    tx_three = to_row(tx.at[1:4], tx.at[1:4], t_send.at[3], t_recv.at[3], me_r)
+    tx_three = to_row(tx.at[1:4], tx.at[1:4], t_send.at[2], t_recv.at[2], me_r)
     tx_three.wait_recv()
     trace[0, 0] = jnp.sum(tx[...]) / (NB * BLK)
     tx_three.wait_send()
@@ -403,8 +396,7 @@
             pltpu.VMEM((32, BLK, BLK), BF),
             pltpu.VMEM((TILES, BLK, BLK), F32),
             pltpu.VMEM((TILES, BLK, BLK), F32),
-            pltpu.VMEM((2, 8, BLK), F32),
-            pltpu.VMEM((8, 8, BLK), F32),
+            pltpu.VMEM((16, 8, BLK), F32),
             pltpu.VMEM((4, 8, BLK), F32),
             pltpu.VMEM((4, 8, BLK), F32),
             dma((3,)),
@@ -413,7 +405,7 @@
             dma((2,)), dma((2,)),
             dma((2,)), dma((2,)),
             dma((2,)), dma((2,)),
-            dma((4,)), dma((4,)),
+            dma((3,)), dma((3,)),
             dma(()),
         ],
         compiler_params=pltpu.CompilerParams(

time: 42.3 us -> 40.7 us (0.962); the launches traced: 41.5 us -> 40.5 us
  Pallas kernels: 37.1 us -> 36 us
    pallas_call x1, Pallas kernels: 37.1 us -> 36 us  [fast_call(): pl.pallas_call(kernel, out_shape=(jax.ShapeDtypeStruct((TILES, BLK, BLK),...]
where the time goes in v4:
time: 40.7 us; the launch traced here: 40.5 us
  Pallas kernels  36 us (88%)
  between operations  3.13 us (8%)
  other arithmetic  1.27 us (3%)
    pallas_call x1, Pallas kernels, fast_call(): pl.pallas_call(kernel, out_shape=(jax.ShapeDtypeStruct((TILES, BLK, BLK),...  36 us
    broadcast_in_dim x1, other arithmetic, per_device(): return (out[None, None], mean_diagonal)  1.26 us

profile of v4, /device:TPU:1, one launch (start us, length us, event | category | flops | bytes accessed | tf_op | source)
XLA Modules:
  0.0 40.5 jit_solution(11338258771235574719)
XLA Ops:
  0.6 36.0 %shard_map.41 = (f32[18,128,128]{2,1,0:T(8,128)S(1)}, f32[2,128,128]{2,1,0:T(8,128)S(1)}, f32[1,1]{1,0:T(1,128)}, s32[1,1]{1,0:T(1,128)}, s32[18]{0:T(128)S(1)}) custom-call(s32[16,16,2,18]{3,2,1,0:T(2,128)} %bitcast.53, f32[18,128,128]{2,1,0:T(8,128)} %bitcast.52), custom_call_target="tpu_custom_call" | custom-call | tf_op jit(solution)/shard_map/pallas_call | solution.py:366
  37.4 1.3 %conditional.1 = (f32[]{:T(128)}, f32[1,1,18,128,128]{4,3,2,1,0:T(8,128)}) conditional(s32[]{:T(128)} %bitcast.32, (f32[1,1]{1,0:T(1,128)}, s32[18]{0:T(128)S(1)}, f32[2,128,128]{2,1,0:T(8,128)S(1)}, f32[18,128,128]{2,1,0:T(8,128)S(1)}) %tuple.73, (s32[16,16,18,2]{2,3,1,0:T(2,128)}, f32[1,1,18,128,128]{4,3,2,1,0:T(8,128)}) %tuple.26), branch_computations={%region_0.1_spmd, %region_1.14_spmd} | conditional | flops 2475514112 | bytes 227415104 | solution.py:473
  37.4 1.3 %select_bitcast_fusion = f32[1,1,18,128,128]{4,3,2,1,0:T(8,128)} fusion(f32[18,128,128]{2,1,0:T(8,128)S(1)} %get-tuple-element.38, f32[128,128]{1,0:T(8,128)S(1)} %get-tuple-element.104, f32[128,128]{1,0:T(8,128)S(1)} %get-tuple-element.103, pred[18]{0:T(512)(128)(4,1)S(1)} %get-tuple-element.106, pred[18]{0:T(512)(128)(4,1)S(1)} %get-tuple-element.105), kind=kLoop, calls=%fused_computation.3 | loop fusion | flops 589824 | bytes 2490404 | tf_op jit(solution)/shard_map/broadcast_in_dim | solution.py:479
  (2 shorter events, 0.0 us)

commit v5 on v4

--- a/solution.py
+++ b/solution.py
@@ -298,13 +298,13 @@
     spread_twin(dpack, d_send, d_recv).start()
     expand_half(dpack, 0, dfull)
 
-    reduce_send(1)
-
     tcol_all = to_col(tcol.at[1:16], tcol.at[1:16], t_send.at[0], t_recv.at[0], twin)
     tcol_all.wait_recv()
     tz[0] = jnp.sum(tcol[...], axis=0)
     for b in (1, 2, 3):
         to_row(tz.at[0], tz.at[RING_BACK[b]], t_send.at[1], t_recv.at[1], zs[b]).start()
+
+    reduce_send(1)
 
     spread_twin(dpack, d_send, d_recv).wait_recv()
     expand_half(dpack, 1, dfull)

time: 40.7 us -> 38 us (0.934)
  Pallas kernels: 36 us -> 33.3 us
    pallas_call x1, Pallas kernels: 36 us -> 33.3 us  [fast_call(): pl.pallas_call(kernel, out_shape=(jax.ShapeDtypeStruct((TILES, BLK, BLK),...]
where the time goes in v5:
time: 38 us; the launch traced here: 37.8 us
  Pallas kernels  33.3 us (88%)
  between operations  3.13 us (8%)
  other arithmetic  1.27 us (3%)
    pallas_call x1, Pallas kernels, fast_call(): pl.pallas_call(kernel, out_shape=(jax.ShapeDtypeStruct((TILES, BLK, BLK),...  33.3 us
    broadcast_in_dim x1, other arithmetic, per_device(): return (out[None, None], mean_diagonal)  1.26 us

profile of v5, /device:TPU:1, one launch (start us, length us, event | category | flops | bytes accessed | tf_op | source)
XLA Modules:
  0.0 37.8 jit_solution(12926547374018596221)
XLA Ops:
  0.6 33.3 %shard_map.41 = (f32[18,128,128]{2,1,0:T(8,128)S(1)}, f32[2,128,128]{2,1,0:T(8,128)S(1)}, f32[1,1]{1,0:T(1,128)}, s32[1,1]{1,0:T(1,128)}, s32[18]{0:T(128)S(1)}) custom-call(s32[16,16,2,18]{3,2,1,0:T(2,128)} %bitcast.53, f32[18,128,128]{2,1,0:T(8,128)} %bitcast.52), custom_call_target="tpu_custom_call" | custom-call | tf_op jit(solution)/shard_map/pallas_call | solution.py:366
  34.7 1.3 %conditional.1 = (f32[]{:T(128)}, f32[1,1,18,128,128]{4,3,2,1,0:T(8,128)}) conditional(s32[]{:T(128)} %bitcast.32, (f32[1,1]{1,0:T(1,128)}, s32[18]{0:T(128)S(1)}, f32[2,128,128]{2,1,0:T(8,128)S(1)}, f32[18,128,128]{2,1,0:T(8,128)S(1)}) %tuple.73, (s32[16,16,18,2]{2,3,1,0:T(2,128)}, f32[1,1,18,128,128]{4,3,2,1,0:T(8,128)}) %tuple.26), branch_computations={%region_0.1_spmd, %region_1.14_spmd} | conditional | flops 2475514112 | bytes 227415104 | solution.py:473
  34.7 1.3 %select_bitcast_fusion = f32[1,1,18,128,128]{4,3,2,1,0:T(8,128)} fusion(f32[18,128,128]{2,1,0:T(8,128)S(1)} %get-tuple-element.38, f32[128,128]{1,0:T(8,128)S(1)} %get-tuple-element.104, f32[128,128]{1,0:T(8,128)S(1)} %get-tuple-element.103, pred[18]{0:T(512)(128)(4,1)S(1)} %get-tuple-element.106, pred[18]{0:T(512)(128)(4,1)S(1)} %get-tuple-element.105), kind=kLoop, calls=%fused_computation.3 | loop fusion | flops 589824 | bytes 2490404 | tf_op jit(solution)/shard_map/broadcast_in_dim | solution.py:479
  (2 shorter events, 0.0 us)
